TPU v7x, 512 devices: a whole 4x4x16 slice. The times are simulated.
512 devices in a mesh: dp: 32 (over x_lo, z), ctx: 16 (over x_hi, y, core).
Axes of the slice: x: 4 (x_hi: 2, x_lo: 2; x = x_hi * 2 + x_lo), y: 4, z: 16, core: 2. Of those that a mesh axis runs over, the one named last changes fastest.
Arguments:
- hidden_in: bfloat16 [32, 2048, 2560], P('dp', 'ctx'), may hold values from -6 to 6
- queries: bfloat16 [32, 2048, 2048], P('dp', 'ctx'), may hold values from -6 to 6
- keys_values: bfloat16 [32, 2048, 1024], P('dp', 'ctx'), may hold values from -6 to 6
- attn_out: bfloat16 [32, 2048, 2048], P('dp', 'ctx'), may hold values from -2 to 2
- out_grad: bfloat16 [32, 2048, 2048], P('dp', 'ctx'), may hold values from -6 to 6
- log_norms: float32 [32, 16, 2048], P('dp', None, 'ctx')
- proj_in: bfloat16 [2560, 64], replicated, may hold values from -0.125 to 0.125
- proj_q: bfloat16 [2048, 64], replicated, may hold values from -0.125 to 0.125
- proj_k: bfloat16 [512, 64], replicated, may hold values from -0.25 to 0.25
- proj_v: bfloat16 [512, 64], replicated, may hold values from -0.25 to 0.25
- query_docs: int32 [8], replicated, may hold values from 0 to 31
Outputs:
- unit_grads: float32 [32, 12288], P('dp')
- scores: float32 [32, 8], P('dp')
All inputs are finite; a program needn't handle non-finite values.
Results may differ from a plain program's by a relative error of at most 0.0041.
Values may be sent and summed in bfloat16 or wider, within the bound.
No kernel may reach another device: no remote copies, remote signals or barrier semaphores. Data moves between devices by JAX's collectives and lax.ppermute only.
A program may use at most 128 MiB of HBM per device.

v0:
```python
import jax
import jax.numpy as jnp
from jax import lax
from jax.sharding import PartitionSpec as P

KV_HEADS = 4
HEAD_DIM = 128
RANK = 64


def local(
    hidden_in,
    queries,
    keys_values,
    attn_out,
    out_grad,
    log_norms,
    proj_in,
    proj_q,
    proj_k,
    proj_v,
    query_docs,
):
    high = lax.Precision.HIGHEST
    tok = queries.shape[1]
    heads = log_norms.shape[1]
    group = heads // KV_HEADS
    kv_cols = KV_HEADS * HEAD_DIM
    scale = HEAD_DIM ** (-0.5)
    first = lax.axis_index("ctx") * tok
    inputs_p = jnp.dot(hidden_in[0], proj_in, preferred_element_type=jnp.float32).astype(
        jnp.bfloat16
    )
    q_heads = queries[0].reshape(tok, KV_HEADS, group, HEAD_DIM).transpose(1, 2, 0, 3)
    d_heads = out_grad[0].reshape(tok, KV_HEADS, group, HEAD_DIM).transpose(1, 2, 0, 3)
    o_heads = attn_out[0].reshape(tok, KV_HEADS, group, HEAD_DIM).transpose(1, 2, 0, 3)
    delta = jnp.einsum("kgtd,kgtd->kgt", d_heads, o_heads, preferred_element_type=jnp.float32)
    lse = log_norms[0].reshape(KV_HEADS, group, tok)
    proj_k32 = proj_k.astype(jnp.float32)
    proj_v32 = proj_v.astype(jnp.float32)
    piece = lax.all_gather(keys_values[0], "ctx", axis=0, tiled=True)
    count = piece.shape[0]
    key_part = piece[:, :kv_cols].reshape(count, KV_HEADS, HEAD_DIM).transpose(1, 0, 2)
    value_part = piece[:, kv_cols:].reshape(count, KV_HEADS, HEAD_DIM).transpose(1, 0, 2)
    q_pos = first + jnp.arange(tok, dtype=jnp.int32)
    k_pos = jnp.arange(count, dtype=jnp.int32)
    visible = k_pos[None, :] <= q_pos[:, None]

    def one_group(args):
        q_grp, d_grp, l_grp, e_grp, k_grp, v_grp = args
        raw = jnp.einsum("gtd,cd->gtc", q_grp, k_grp, preferred_element_type=jnp.float32) * scale
        probs = jnp.exp(jnp.where(visible[None], raw - l_grp[:, :, None], -1e30))
        dprobs = jnp.einsum("gtd,cd->gtc", d_grp, v_grp, preferred_element_type=jnp.float32)
        dscores = probs * (dprobs - e_grp[:, :, None])
        probs_b = probs.astype(jnp.bfloat16)
        dscores_b = dscores.astype(jnp.bfloat16)
        grad_v = jnp.einsum("gtc,gtd->cd", probs_b, d_grp, preferred_element_type=jnp.float32)
        grad_k = (
            jnp.einsum("gtc,gtd->cd", dscores_b, q_grp, preferred_element_type=jnp.float32) * scale
        )
        grad_q = (
            jnp.einsum("gtc,cd->gtd", dscores_b, k_grp, preferred_element_type=jnp.float32) * scale
        )
        return (grad_q, grad_k, grad_v)

    grad_q, grad_k, grad_v = lax.map(
        one_group, (q_heads, d_heads, lse, delta, key_part, value_part)
    )
    grad_k = grad_k.transpose(1, 0, 2).reshape(count, kv_cols)
    grad_v = grad_v.transpose(1, 0, 2).reshape(count, kv_cols)
    terms = jnp.concatenate(
        [jnp.dot(grad_k, proj_k32, precision=high), jnp.dot(grad_v, proj_v32, precision=high)],
        axis=1,
    )
    grad_q, terms = (grad_q, terms)
    mine = lax.psum_scatter(terms, "ctx", scatter_dimension=0, tiled=True)
    kv_part = jnp.dot(inputs_p.astype(jnp.float32).T, mine, precision=high)
    dq_rows = grad_q.transpose(2, 0, 1, 3).reshape(tok, heads * HEAD_DIM)
    dq_proj = jnp.dot(dq_rows, proj_q.astype(jnp.float32), precision=high)
    q_part = jnp.dot(inputs_p.astype(jnp.float32).T, dq_proj, precision=high)
    local_grad = jnp.concatenate([q_part, kv_part], axis=1)
    doc_grad = lax.psum(local_grad, "ctx").reshape(1, -1)
    unit = doc_grad / jnp.sqrt(jnp.mean(doc_grad * doc_grad) + 1e-06)
    every = lax.all_gather(unit.astype(jnp.bfloat16), "dp", axis=0, tiled=True).astype(unit.dtype)
    chosen = jnp.take(every, query_docs, axis=0)
    scores = jnp.dot(unit, chosen.T, precision=high) / (3.0 * RANK * RANK)
    return (unit, scores)


def solution(mesh):
    in_specs = (
        P("dp", "ctx", None),
        P("dp", "ctx", None),
        P("dp", "ctx", None),
        P("dp", "ctx", None),
        P("dp", "ctx", None),
        P("dp", None, "ctx"),
        P(),
        P(),
        P(),
        P(),
        P(),
    )
    out_specs = (P("dp", None), P("dp", None))
    return jax.shard_map(local, mesh=mesh, in_specs=in_specs, out_specs=out_specs, check_vma=False)
```

profile of v0, /device:TPU:4, one launch (start us, length us, event | category | flops | bytes accessed | tf_op | source)
XLA Modules:
  0.0 411.2 jit_solution(13713937765726623171)
XLA Ops:
  7.2 1.9 copy.30
  9.2 2.1 copy.29
  14.5 70.7 %all-gather.4.cloned.1.call-done = bf16[1,2048,1024]{1,2,0:T(8,128)(2,1)} async-done(((bf16[1,128,1024]{1,2,0:T(8,128)(2,1)}), bf16[1,2048,1024]{1,2,0:T(8,128)(2,1)}) %all-gather.4.cloned.1.call-update) | async-done | bytes 4194320 | tf_op jit(solution)/shard_map/all_gather | solution.py:41
  85.2 4.1 %fusion.35 = (bf16[2048,512]{0,1:T(8,128)(2,1)}, bf16[2048,512]{0,1:T(8,128)(2,1)S(1)}) fusion(bf16[2048,1024]{0,1:T(8,128)(2,1)} %bitcast.137), kind=kLoop, calls=%fused_computation.58 | loop fusion | bytes 8388608 | tf_op jit(solution)/shard_map/slice | solution.py:44
  89.4 74.6 %while.15 = (s32[]{:T(128)}, f32[4,4,128,128]{2,3,1,0:T(8,128)}, f32[4,2048,128]{1,2,0:T(8,128)}, f32[4,2048,128]{1,2,0:T(8,128)}, bf16[4,4,128,128]{2,3,1,0:T(8...) while((s32[]{:T(128)}, f32[4,4,128,128]{2,3,1,0:T(8,128)}, ...), condition=%wide.region_1.2_spmd.clone, body=%wide.region_0.1_spmd.clone.sunk | while | flops 1350107136 | bytes 66862876 | solution.py:66
  90.3 2.2 select_exponential_fusion.2
  92.5 1.9 copy-done.1
  94.5 1.8 multiply_convert_fusion.2
  98.9 2.7 fusion.81
  104.2 3.8 fusion.82
  109.0 2.2 select_exponential_fusion.2
  111.2 1.9 copy-done.1
  113.1 1.8 multiply_convert_fusion.2
  117.5 2.7 fusion.81
  122.9 3.7 fusion.82
  127.6 2.2 select_exponential_fusion.2
  129.8 1.9 copy-done.1
  131.7 1.8 multiply_convert_fusion.2
  133.5 1.8 fusion.80
  136.1 2.7 fusion.81
  141.5 3.8 fusion.82
  146.2 2.2 select_exponential_fusion.2
  148.4 1.9 copy-done.1
  150.3 1.8 multiply_convert_fusion.2
  152.1 1.8 fusion.80
  154.8 2.7 fusion.81
  160.1 3.8 fusion.82
  163.9 4.0 fusion.39
  168.0 1.8 fusion.38
  172.0 88.7 %reduce-scatter.2.cloned.1.call-done = f32[128,128]{0,1:T(8,128)} async-done(((f32[2048,128]{0,1:T(8,128)}), f32[128,128]{0,1:T(8,128)}) %reduce-scatter.2.cloned.1.call-update) | async-done | bytes 65552 | tf_op jit(solution)/shard_map/reduce_scatter | solution.py:76
  261.8 65.5 %psum.7 = f32[64,192]{1,0:T(8,128)S(1)} all-reduce(f32[64,192]{1,0:T(8,128)S(1)} %pad_maximum_fusion.1), channel_id=1, replica_groups=mesh['dp'=32,'ctx'=16] {'ctx'}, use_global_device_ids=true, to_apply=%region_3.4 | all-reduce | flops 12288 | bytes 98304 | tf_op jit(solution)/shard_map/psum | solution.py:82
  328.9 72.3 %all-gather.1 = bf16[32,1,12288]{2,1,0:T(2,128)(2,1)S(1)} all-gather(bf16[1,1,12288]{2,1,0:T(2,128)(2,1)S(1)} %convert_bitcast_fusion), channel_id=1, replica_groups=mesh['dp'=32,'ctx'=16] {'dp'}, dimensions={0}, use_global_device_ids=true | all-gather | bytes 811008 | tf_op jit(solution)/shard_map/all_gather | solution.py:84
  (112 shorter events, 31.8 us)
Async XLA Ops:
  7.2 163.8 %copy-start = (bf16[1,128,2560]{2,1,0:T(8,128)(2,1)S(1)}, bf16[1,128,2560]{2,1,0:T(8,128)(2,1)}, u32[]{:S(2)}) copy-start(bf16[1,128,2560]{2,1,0:T(8,128)(2,1)} %param.13) | copy-start | bytes 1966084
  7.2 6.0 %copy-start.8 = (bf16[1,128,2048]{2,1,0:T(8,128)(2,1)S(1)}, bf16[1,128,2048]{2,1,0:T(8,128)(2,1)}, u32[]{:S(2)}) copy-start(bf16[1,128,2048]{2,1,0:T(8,128)(2,1)} %param.16) | copy-start | bytes 1572868
  7.2 78.0 %all-gather.4.cloned.1.call-start = ((), (), s32[]{:S(2)}) async-start(), calls=%async_computation.2 | async-start | bytes 4456448 | tf_op jit(solution)/shard_map/all_gather | solution.py:41
  9.2 251.5 %reduce-scatter.2.cloned.1.call-start = ((), (), s32[]{:S(2)}) async-start(), calls=%async_computation.1 | async-start | bytes 1114112 | tf_op jit(solution)/shard_map/reduce_scatter | solution.py:76
  89.4 74.6 %copy-start.12 = (bf16[512,64]{0,1:T(8,128)(2,1)S(1)}, bf16[512,64]{0,1:T(8,128)(2,1)}, u32[]{:S(2)}) copy-start(bf16[512,64]{0,1:T(8,128)(2,1)} %param.22) | copy-start | bytes 196612
  89.4 3.2 copy-start.2
  89.4 3.2 copy-start.4
  92.5 2.0 copy-start.1
  98.9 5.3 %copy-start.5 = (bf16[4,4,128,128]{2,3,1,0:T(8,128)(2,1)S(1)}, bf16[4,4,128,128]{2,3,1,0:T(8,128)(2,1)}, u32[]{:S(2)}) copy-start(bf16[4,4,128,128]{2,3,1,0:T(8,128)(2,1)} %copy-done.4) | copy-start | bytes 1572868 | tf_op jit(solution)/shard_map/while
  104.2 3.8 copy-start.3
  108.1 3.1 copy-start.2
  108.1 3.1 copy-start.4
  111.2 2.0 copy-start.1
  117.5 5.4 %copy-start.5 = (bf16[4,4,128,128]{2,3,1,0:T(8,128)(2,1)S(1)}, bf16[4,4,128,128]{2,3,1,0:T(8,128)(2,1)}, u32[]{:S(2)}) copy-start(bf16[4,4,128,128]{2,3,1,0:T(8,128)(2,1)} %copy-done.4) | copy-start | bytes 1572868 | tf_op jit(solution)/shard_map/while
  122.9 3.8 copy-start.3
  126.7 3.1 copy-start.2
  126.7 3.1 copy-start.4
  129.7 2.0 copy-start.1
  136.1 5.4 %copy-start.5 = (bf16[4,4,128,128]{2,3,1,0:T(8,128)(2,1)S(1)}, bf16[4,4,128,128]{2,3,1,0:T(8,128)(2,1)}, u32[]{:S(2)}) copy-start(bf16[4,4,128,128]{2,3,1,0:T(8,128)(2,1)} %copy-done.4) | copy-start | bytes 1572868 | tf_op jit(solution)/shard_map/while
  141.5 3.8 copy-start.3
  145.3 3.1 copy-start.2
  145.3 3.1 copy-start.4
  148.3 2.0 copy-start.1
  154.7 5.4 %copy-start.5 = (bf16[4,4,128,128]{2,3,1,0:T(8,128)(2,1)S(1)}, bf16[4,4,128,128]{2,3,1,0:T(8,128)(2,1)}, u32[]{:S(2)}) copy-start(bf16[4,4,128,128]{2,3,1,0:T(8,128)(2,1)} %copy-done.4) | copy-start | bytes 1572868 | tf_op jit(solution)/shard_map/while
  160.1 3.8 copy-start.3
  163.9 4.1 copy-start.6
  163.9 4.1 copy-start.13
  168.0 2.9 copy-start.14
  168.0 3.0 copy-start.9
  168.0 3.3 copy-start.7
  168.0 3.3 copy-start.10
  328.7 74.1 %copy-start.11 = (f32[1,12288]{1,0:T(1,128)}, f32[1,12288]{1,0:T(1,128)S(1)}, u32[]{:S(2)}) copy-start(f32[1,12288]{1,0:T(1,128)S(1)} %div.36) | copy-start | bytes 147460
Sparse Core Ops, SparseCore 0:
  11.2 74.0 all-gather.3
  171.0 89.6 reduce-scatter.1
where the time goes:
time: 412 us; the launch traced here: 411 us
  waiting for transfers between devices  159 us (39%)
  blocking collectives  138 us (33%)
  matrix products  58.2 us (14%)
  local copies, waits for them, and re-layouts  35.9 us (9%)
  between operations  15 us (4%)
  other arithmetic  4.44 us (1%)
    reduce_scatter x1, waiting for transfers between devices, local(): mine = lax.psum_scatter(terms, 'ctx', scatter_dimension=0, tiled=True)  88.7 us
    all_gather x1, blocking collectives, local(): lax.all_gather(unit.astype(jnp.bfloat16), 'dp', axis=0, tiled=True)  72.3 us
    all_gather x1, waiting for transfers between devices, local(): piece = lax.all_gather(keys_values[0], 'ctx', axis=0, tiled=True)  70.7 us
    psum x1, blocking collectives, local(): doc_grad = lax.psum(local_grad, 'ctx').reshape(1, -1)  65.5 us
    dot_general x4, matrix products, one_group(): jnp.einsum('gtc,gtd->cd', probs_b, d_grp, preferred_element_type=jnp.floa...  15.1 us
    dynamic_update_slice x16, local copies, waits for them, and re-layouts, local(): lax.map(one_group, (q_heads, d_heads, lse, delta, key_part, value_part))  14 us
    dot_general x4, matrix products, one_group(): jnp.einsum('gtc,gtd->cd', dscores_b, q_grp, preferred_element_type=jnp.fl...  10.8 us
    dot_general x4, matrix products, one_group(): jnp.einsum('gtd,cd->gtc', q_grp, k_grp, preferred_element_type=jnp.float32)  8.64 us
  transfers between devices with their start and end apart: 2, of which 2 were waited for; matrix products, arithmetic and copies ran while one was open for 2% of the time, Pallas kernels for 0%

commit v1 on v0

v1 whole, which is shorter than its diff:
```python
import functools
import math

import jax
import jax.numpy as jnp
from jax import lax
from jax.experimental import pallas as pl
from jax.experimental.pallas import tpu as pltpu
from jax.sharding import PartitionSpec as P

KV_HEADS = 4
HEAD_DIM = 128
RANK = 64
LANES = 128
SCALE = HEAD_DIM ** (-0.5)
F32 = jnp.float32
BF16 = jnp.bfloat16
VMEM = pl.BlockSpec(memory_space=pltpu.VMEM)
SMEM = pl.BlockSpec(memory_space=pltpu.SMEM)

Q_AT, D_AT, K_AT, V_AT, X_AT, WIDE = 0, 256, 512, 640, 768, 896


def nt(a, b):
    return lax.dot_general(a, b, (((1,), (1,)), ((), ())), preferred_element_type=F32)


def tn(a, b):
    return lax.dot_general(a, b, (((0,), (0,)), ((), ())), preferred_element_type=F32)


def nn(a, b):
    return jnp.dot(a, b, preferred_element_type=F32)


def split2(a):
    high = a.astype(BF16)
    return high, (a - high.astype(F32)).astype(BF16)


def lane_of(shape):
    return lax.broadcasted_iota(jnp.int32, shape, len(shape) - 1)


def row_of(shape):
    return lax.broadcasted_iota(jnp.int32, shape, len(shape) - 2)


def message_kernel(h_ref, q_ref, kv_ref, o_ref, d_ref, lse_ref, pin_ref, msg_ref):
    tok = q_ref.shape[0]
    heads = lse_ref.shape[0]
    chips = heads // 2
    group = heads // KV_HEADS
    x = nn(h_ref[...], pin_ref[...])
    x = jnp.concatenate([x, jnp.zeros((tok, LANES - RANK), F32)], axis=1)
    lse = jnp.concatenate([lse_ref[...], jnp.zeros((LANES - heads, tok), F32)], axis=0)
    terms = lse.T * (-1.0 / SCALE)
    lane = lane_of((tok, LANES))
    for h in range(heads):
        cols = slice(h * HEAD_DIM, (h + 1) * HEAD_DIM)
        prod = d_ref[:, cols].astype(F32) * o_ref[:, cols].astype(F32)
        delta = jnp.sum(prod, axis=1, keepdims=True)
        terms = jnp.where(lane == heads + h, -delta, terms)
    high, rest = terms.astype(BF16), None
    rest = terms - high.astype(F32)
    mid = rest.astype(BF16)
    low = (rest - mid.astype(F32)).astype(BF16)
    src = row_of((LANES, chips * LANES))
    dst = lane_of((LANES, chips * LANES))
    head = src % heads
    place = (head // 2) * LANES + RANK + (src // heads) * 6 + (head % 2) * 3
    place = jnp.where(src < 2 * heads, place, -8)
    spread = jnp.zeros((tok, chips * LANES), F32)
    for j, part in enumerate((high, mid, low)):
        pick = jnp.where(dst == place + j, 1.0, 0.0).astype(BF16)
        spread = spread + nn(part, pick)
    for p in range(chips):
        two = slice(p * 2 * HEAD_DIM, (p + 1) * 2 * HEAD_DIM)
        kv = 2 * p // group
        kv_cols = KV_HEADS * HEAD_DIM
        msg_ref[p, :, Q_AT:D_AT] = q_ref[:, two]
        msg_ref[p, :, D_AT:K_AT] = d_ref[:, two]
        msg_ref[p, :, K_AT:V_AT] = kv_ref[:, kv * HEAD_DIM : (kv + 1) * HEAD_DIM]
        msg_ref[p, :, V_AT:X_AT] = kv_ref[:, kv_cols + kv * HEAD_DIM : kv_cols + (kv + 1) * HEAD_DIM]
        block = x + spread[:, p * LANES : (p + 1) * LANES]
        msg_ref[p, :, X_AT:WIDE] = block.astype(BF16)


def attention_kernel(
    at_ref, r_ref, o_ref, pq_ref, pk_ref, pv_ref, out_ref,
    qs, ds, qp, dp_, kp, vp, wa, wb, ps, dss, gq, gk, gv,
):
    chip = at_ref[0]
    core = at_ref[1]
    blocks, tok, _ = r_ref.shape
    rows = blocks * tok
    half = 2 * tok
    groups = rows // half
    group = pk_ref.shape[0] // HEAD_DIM
    heads = pq_ref.shape[0] // HEAD_DIM
    per_kv = heads // group

    def part(ref, at):
        return ref[:, :, at : at + LANES].reshape(rows, LANES)

    lane = lane_of((rows, LANES))
    xl = part(r_ref, X_AT)
    none = jnp.zeros_like(xl)
    kv = (2 * chip) // per_kv
    pk = pk_ref[pl.ds(pl.multiple_of(kv * HEAD_DIM, HEAD_DIM), HEAD_DIM), :]
    pv = pv_ref[pl.ds(pl.multiple_of(kv * HEAD_DIM, HEAD_DIM), HEAD_DIM), :]
    pk = jnp.concatenate([pk, pk], axis=1)
    pv = jnp.concatenate([pv, pv], axis=1)
    first = lane < RANK

    def doubled(a, proj):
        full = nn(a, proj)
        high = full.astype(BF16).astype(F32)
        return jnp.where(first, high, full - high).astype(BF16)

    for h in range(2):
        q = part(r_ref, Q_AT + h * LANES)
        d = part(r_ref, D_AT + h * LANES)
        for ref, val, kind in ((qs, q, 0), (ds, d, 1)):
            start = RANK + kind * 6 + h * 3
            mask = (lane >= start) & (lane < start + 3)
            side = jnp.where(mask, xl, none)
            for g in range(groups):
                ref[g, h * half : (h + 1) * half, :LANES] = val[g * half : (g + 1) * half]
                ref[g, h * half : (h + 1) * half, LANES:] = side[g * half : (g + 1) * half]
        qp[h] = doubled(q, pk)
        dp_[h] = doubled(d, pv)

    ones = jnp.ones((rows, LANES), BF16)
    kp[:, LANES:] = ones
    vp[:, LANES:] = ones
    gq[...] = jnp.zeros_like(gq)
    gk[...] = jnp.zeros_like(gk)
    gv[...] = jnp.zeros_like(gv)
    r_io = row_of((2 * half, half)) % half
    c_io = lane_of((2 * half, half))
    own_seen = c_io <= r_io
    other_seen = (c_io // tok) < (r_io // tok) + core
    fold = SCALE * math.log2(math.e)

    for src, base, seen in ((r_ref, 0, own_seen), (o_ref, K_AT, other_seen)):
        key = part(src, K_AT - base)
        x_key = part(src, X_AT - base)
        kp[:, :LANES] = key
        vp[:, :LANES] = part(src, V_AT - base)
        for h, w in enumerate((wa, wb)):
            at = pl.multiple_of((2 * chip + h) * HEAD_DIM, HEAD_DIM)
            pq = pq_ref[pl.ds(at, HEAD_DIM), :]
            w[:, :LANES] = doubled(key, jnp.concatenate([pq, pq], axis=1))
            w[:, LANES:] = x_key
        for g in range(groups):
            upto = (g + 1) * half
            for n in range(g + 1):
                cols = slice(n * half, (n + 1) * half)
                s = nt(qs[g], kp[cols, :])
                probs = jnp.exp2(s * fold)
                if n == g:
                    probs = jnp.where(seen, probs, 0.0)
                dscores = probs * nt(ds[g], vp[cols, :])
                ps[:, cols] = probs.astype(BF16)
                dss[:, cols] = dscores.astype(BF16)
            acc_v = nn(ps[:, :upto], wa[:upto, LANES:])
            here = slice(g * half, (g + 1) * half)
            for h, w in enumerate((wa, wb)):
                mine = slice(h * half, (h + 1) * half)
                acc = nn(dss[mine, :upto], w[:upto, :])
                high, low = split2(acc)
                vh, vl = split2(acc_v[mine])
                xq = r_ref[2 * g : 2 * g + 2, :, X_AT:WIDE].reshape(half, LANES)
                gq[...] += tn(xq, jnp.concatenate([high[:, :LANES], low[:, :LANES]], axis=1))
                gk[...] += tn(qp[h, here, :], jnp.concatenate([high[:, LANES:], low[:, LANES:]], axis=1))
                gv[...] += tn(dp_[h, here, :], jnp.concatenate([vh, vl], axis=1))

    def quarter(a):
        t = a[:, :LANES] + a[:, LANES:]
        return t

    tq = quarter(gq[:RANK, :])
    out_q = (tq + pltpu.roll(tq, RANK, 1)) * SCALE
    tk = quarter(gk[:RANK, :] + gk[RANK:, :])
    tv = quarter(gv[:RANK, :] + gv[RANK:, :])
    zero = jnp.zeros((RANK, LANES), F32)
    tk = jnp.concatenate([tk, zero], axis=0).T[:RANK] * SCALE
    tv = jnp.concatenate([tv, zero], axis=0).T[:RANK]
    low_lanes = lane_of((RANK, LANES)) < RANK
    top = jnp.where(low_lanes, out_q, pltpu.roll(tk, RANK, 1))
    bottom = jnp.where(
        lane_of((RANK // 2, LANES)) < RANK, tv[: RANK // 2], pltpu.roll(tv, RANK, 1)[RANK // 2 :]
    )
    packed = jnp.concatenate([top, bottom], axis=0).astype(BF16)
    for i in range(out_ref.shape[0]):
        out_ref[i] = packed


def unit_kernel(at_ref, parts_ref, unit_ref, mine_ref, send_ref, flat):
    total = parts_ref[0].astype(F32)
    for i in range(1, parts_ref.shape[0]):
        total = total + parts_ref[i].astype(F32)
    mean = jnp.sum(total * total) / (3.0 * RANK * RANK)
    unit = total / jnp.sqrt(jnp.full((1, LANES), mean, F32) + 1e-6)
    unit_ref[:, :LANES] = unit[:RANK]
    unit_ref[: RANK // 2, LANES:] = unit[RANK:, :RANK]
    unit_ref[RANK // 2 :, LANES:] = unit[RANK:, RANK:]
    flat[...] = jnp.zeros_like(flat)
    flat[: unit.shape[0], :] = unit
    depth = mine_ref.shape[0]
    mine = flat[pl.ds(pl.multiple_of(at_ref[0] * depth, depth), depth), :]
    mine_ref[...] = mine
    send = mine.astype(BF16)
    for i in range(send_ref.shape[0]):
        send_ref[i] = send


def score_kernel(docs_ref, mine_ref, every_ref, out_ref):
    mine = mine_ref[...]
    count = docs_ref.shape[0]
    lane = lane_of((1, LANES))
    res = jnp.zeros((1, LANES), F32)
    for q in range(count):
        other = every_ref[docs_ref[q]].astype(F32)
        res = jnp.where(lane == q, jnp.sum(mine * other), res)
    for i in range(out_ref.shape[0]):
        out_ref[i] = res


def local(
    hidden_in, queries, keys_values, attn_out, out_grad, log_norms, proj_in, proj_q, proj_k, proj_v, query_docs
):
    tok = queries.shape[1]
    heads = log_norms.shape[1]
    chips = heads // 2
    docs = lax.axis_size("dp")
    same_core = [[2 * p + c for p in range(chips)] for c in range(2)]
    index = lax.axis_index("ctx")
    at = jnp.stack([index // 2, index % 2]).astype(jnp.int32)
    params = pltpu.CompilerParams(vmem_limit_bytes=40 * 2**20)

    with jax.named_scope("message"):
        msg = pl.pallas_call(
            message_kernel,
            out_shape=jax.ShapeDtypeStruct((chips, tok, WIDE), BF16),
            in_specs=[VMEM] * 7,
            out_specs=VMEM,
            compiler_params=params,
        )(hidden_in[0], queries[0], keys_values[0], attn_out[0], out_grad[0], log_norms[0], proj_in)
    with jax.named_scope("exchange_heads"):
        got = lax.all_to_all(msg, "ctx", 0, 0, axis_index_groups=same_core, tiled=True)
    with jax.named_scope("swap_cores"):
        other = lax.ppermute(got[:, :, K_AT:], "ctx", [(i, i ^ 1) for i in range(2 * chips)])
    rows = chips * tok
    half = 2 * tok
    groups = rows // half
    with jax.named_scope("attention"):
        partial = pl.pallas_call(
            attention_kernel,
            out_shape=jax.ShapeDtypeStruct((2 * chips, 3 * RANK // 2, LANES), BF16),
            in_specs=[SMEM] + [VMEM] * 5,
            out_specs=VMEM,
            scratch_shapes=[
                pltpu.VMEM((groups, 2 * half, 2 * LANES), BF16),
                pltpu.VMEM((groups, 2 * half, 2 * LANES), BF16),
                pltpu.VMEM((2, rows, LANES), BF16),
                pltpu.VMEM((2, rows, LANES), BF16),
                pltpu.VMEM((rows, 2 * LANES), BF16),
                pltpu.VMEM((rows, 2 * LANES), BF16),
                pltpu.VMEM((rows, 2 * LANES), BF16),
                pltpu.VMEM((rows, 2 * LANES), BF16),
                pltpu.VMEM((2 * half, rows), BF16),
                pltpu.VMEM((2 * half, rows), BF16),
                pltpu.VMEM((LANES, 2 * LANES), F32),
                pltpu.VMEM((LANES, 2 * LANES), F32),
                pltpu.VMEM((LANES, 2 * LANES), F32),
            ],
            compiler_params=params,
        )(at, got, other, proj_q, proj_k, proj_v)
    with jax.named_scope("sum_parts"):
        parts = lax.all_to_all(partial, "ctx", 0, 0, tiled=True)
    with jax.named_scope("unit"):
        unit, mine, send = pl.pallas_call(
            unit_kernel,
            out_shape=(
                jax.ShapeDtypeStruct((RANK, 3 * RANK), F32),
                jax.ShapeDtypeStruct((16, LANES), F32),
                jax.ShapeDtypeStruct((docs, 16, LANES), BF16),
            ),
            in_specs=[SMEM, VMEM],
            out_specs=(VMEM, VMEM, VMEM),
            scratch_shapes=[pltpu.VMEM((16 * chips, LANES), F32)],
        )(at, parts)
    with jax.named_scope("exchange_documents"):
        every = lax.all_to_all(send, "dp", 0, 0, tiled=True)
    with jax.named_scope("score"):
        terms = pl.pallas_call(
            score_kernel,
            out_shape=jax.ShapeDtypeStruct((chips, 1, LANES), F32),
            in_specs=[SMEM, VMEM, VMEM],
            out_specs=VMEM,
        )(query_docs, mine, every)
    with jax.named_scope("sum_scores"):
        terms = lax.all_to_all(terms, "ctx", 0, 0, axis_index_groups=same_core, tiled=True)
    scores = jnp.sum(terms[:, :, : query_docs.shape[0]], axis=0) / (3.0 * RANK * RANK)
    return (unit.reshape(1, -1), scores)


def solution(mesh):
    in_specs = (
        P("dp", "ctx", None),
        P("dp", "ctx", None),
        P("dp", "ctx", None),
        P("dp", "ctx", None),
        P("dp", "ctx", None),
        P("dp", None, "ctx"),
        P(),
        P(),
        P(),
        P(),
        P(),
    )
    out_specs = (P("dp", None), P("dp", None))
    return jax.shard_map(local, mesh=mesh, in_specs=in_specs, out_specs=out_specs, check_vma=False)
```

time: 412 us -> 119 us (0.29)
  the two profiles are of different devices: /device:TPU:4 before, /device:TPU:1 now
where the time goes in v1:
time: 119 us; the launch traced here: 117 us
  blocking collectives  73.9 us (62%)
  Pallas kernels  15.2 us (13%)
  local copies, waits for them, and re-layouts  10.2 us (9%)
  starting transfers between devices  9.76 us (8%)
  waiting for transfers between devices  6.38 us (5%)
    all_to_all x1, blocking collectives, local(): every = lax.all_to_all(send, 'dp', 0, 0, tiled=True)  30.4 us
    all_to_all x1, blocking collectives, local(): lax.all_to_all(msg, 'ctx', 0, 0, axis_index_groups=same_core, tiled=True)  30.1 us
    all_to_all x1, blocking collectives, local(): parts = lax.all_to_all(partial, 'ctx', 0, 0, tiled=True)  13.4 us
    pallas_call x1, Pallas kernels, local(): pl.pallas_call(attention_kernel, out_shape=jax.ShapeDtypeStruct((2 * chip...  10.9 us
    unnamed x24, local copies, waits for them, and re-layouts  7.67 us
    ppermute x1, starting transfers between devices, local(): lax.ppermute(got[:, :, K_AT:], 'ctx', [(i, i ^ 1) for i in range(2 * chip...  5.78 us
    all_to_all x1, waiting for transfers between devices, local(): lax.all_to_all(terms, 'ctx', 0, 0, axis_index_groups=same_core, tiled=True)  4.94 us
    all_to_all x1, starting transfers between devices, local(): lax.all_to_all(terms, 'ctx', 0, 0, axis_index_groups=same_core, tiled=True)  3.98 us
  transfers between devices with their start and end apart: 2, of which 2 were waited for; matrix products, arithmetic and copies ran while one was open for 2% of the time, Pallas kernels for 0%

profile of v1, /device:TPU:1, one launch (start us, length us, event | category | flops | bytes accessed | tf_op | source)
XLA Modules:
  0.0 116.9 jit_solution(10618569513188569275)
XLA Ops:
  0.6 1.3 %copy.13.pin_ref = bf16[2560,64]{1,0:T(8,128)(2,1)S(1)} copy(bf16[2560,64]{0,1:T(8,128)(2,1)} %param.17) | data formatting | bytes 655360 | tf_op args[6]
  1.9 0.0 copy-start
  1.9 1.1 copy-done
  3.0 1.0 copy-done.1
  4.1 0.0 copy-start.2
  4.1 1.0 copy-done.2
  5.1 1.0 copy-done.3
  6.2 0.9 copy-done.4
  7.1 0.7 copy-done.5
  7.8 0.8 message.1
  8.6 0.0 copy-start.7
  8.6 30.1 %all_to_all.20.r_ref = bf16[8,128,896]{2,1,0:T(8,128)(2,1)S(1)} all-to-all(bf16[8,128,896]{2,1,0:T(8,128)(2,1)S(1)} %message.1), channel_id=1, replica_groups={{0,2,4,6,8,10,12,14},{1,3,5,7,9,11,13,15},{16,18,20,22,24,26,28,30},{17..., dimensions={0} | all-to-all | bytes 3670016 | tf_op jit(solution)/shard_map/exchange_heads/all_to_all | solution.py:252
  38.7 1.0 slice.8
  39.7 5.8 %collective-permute-start = (bf16[8,128,384]{2,1,0:T(8,128)(2,1)}, bf16[8,128,384]{2,1,0:T(8,128)(2,1)S(1)}, u32[]{:S(2)}, u32[]{:S(2)}) collective-permute-start(bf16[8,128,384]{2,1,0:T(8,128)(2,1)} %slice.8), channel_id=1, source_target_pairs={{0,1},{1,0},{2,3},{3,2},{4,5},{5,4},{6,7},{7,6},{8,9},{9,8},{10,11... | collective-permute-start | bytes 2359304 | tf_op jit(solution)/shard_map/swap_cores/ppermute | solution.py:254
  45.5 0.0 copy-done.7
  45.5 0.3 copy.14.pq_ref
  45.8 0.0 copy-done.8
  45.8 0.1 copy.15.pk_ref
  45.9 0.0 copy-done.9
  45.9 0.1 copy.16.pv_ref
  46.1 0.1 pad_add_fusion.at_ref
  46.1 1.4 %collective-permute-done.o_ref = bf16[8,128,384]{2,1,0:T(8,128)(2,1)S(1)} collective-permute-done((bf16[8,128,384]{2,1,0:T(8,128)(2,1)}, bf16[8,128,384]{2,1,0:T(8,128)(2,1)S(1)}, u32[]{:S(2)}, u32[]{:S(2)}) %collective-permute-start) | collective-permute-done | bytes 786464 | tf_op jit(solution)/shard_map/swap_cores/ppermute | solution.py:254
  47.6 10.9 %attention.1 = bf16[16,96,128]{2,1,0:T(8,128)(2,1)S(1)} custom-call(s32[2]{0:T(128)S(1)} %pad_add_fusion.at_ref, bf16[8,128,896]{2,1,0:T(8,128)(2,1)S(1)} %all_to_all.20.r_ref, bf16[8,128,384]{2,1,0:T(8,128)(2,1)S(1)} %collective-permute-done.o_ref, bf16[2048,64]{1,0:T(8,128)(2,1)S(1)} %copy.14.pq_ref, bf16[512,64]{1,0:T(8,128)(2,1)S(1)} %copy.15.pk_ref, ...), custom_call_target="tpu_custom_call" | custom-call | tf_op jit(solution)/shard_map/attention/pallas_call | solution.py:259
  58.5 0.0 copy-done.6
  58.5 13.4 %all_to_all.21.parts_ref = bf16[16,96,128]{2,1,0:T(8,128)(2,1)} all-to-all(bf16[16,96,128]{2,1,0:T(8,128)(2,1)S(1)} %attention.1), channel_id=1, replica_groups=mesh['dp'=32,'ctx'=16] {'ctx'}, dimensions={0} | all-to-all | bytes 786432 | tf_op jit(solution)/shard_map/sum_parts/all_to_all | solution.py:282
  71.9 1.9 %unit.1 = (f32[64,192]{1,0:T(8,128)}, f32[16,128]{1,0:T(8,128)}, bf16[32,16,128]{2,1,0:T(8,128)(2,1)}) custom-call(s32[2]{0:T(128)} %copy-done.6, bf16[16,96,128]{2,1,0:T(8,128)(2,1)} %all_to_all.21.parts_ref), custom_call_target="tpu_custom_call" | custom-call | tf_op jit(solution)/shard_map/unit/pallas_call | solution.py:284
  73.8 30.4 %all_to_all.22.every_ref = bf16[32,16,128]{2,1,0:T(8,128)(2,1)} all-to-all(bf16[32,16,128]{2,1,0:T(8,128)(2,1)} %get-tuple-element.7), channel_id=1, replica_groups=mesh['dp'=32,'ctx'=16] {'dp'}, dimensions={0} | all-to-all | bytes 262144 | tf_op jit(solution)/shard_map/exchange_documents/all_to_all | solution.py:296
  104.2 1.7 %score.1 = f32[8,1,128]{2,1,0:T(1,128)} custom-call(s32[8]{0:T(128)} %docs_ref.1, f32[16,128]{1,0:T(8,128)} %get-tuple-element.6.mine_ref, bf16[32,16,128]{2,1,0:T(8,128)(2,1)} %all_to_all.22.every_ref), custom_call_target="tpu_custom_call" | custom-call | tf_op jit(solution)/shard_map/score/pallas_call | solution.py:298
  105.8 4.0 %all-to-all-start.3 = ((f32[8,1,128]{2,1,0:T(1,128)}), f32[8,1,128]{2,1,0:T(1,128)S(1)}, u32[]{:S(2)}, u32[]{:S(2)}) async-start(f32[8,1,128]{2,1,0:T(1,128)} %score.1), calls=%async_computation.3 | async-start | bytes 8192 | tf_op jit(solution)/shard_map/sum_scores/all_to_all | solution.py:305
  109.8 1.6 %reshape.18 = f32[1,12288]{1,0:T(1,128)} reshape(f32[64,192]{1,0:T(8,128)} %get-tuple-element.5) | data formatting | bytes 98304 | tf_op jit(solution)/shard_map/reshape | solution.py:307
  111.4 4.9 %all-to-all-done.3 = f32[8,1,128]{2,1,0:T(1,128)S(1)} async-done(((f32[8,1,128]{2,1,0:T(1,128)}), f32[8,1,128]{2,1,0:T(1,128)S(1)}, u32[]{:S(2)}, u32[]{:S(2)}) %all-to-all-start.3) | async-done | bytes 4128 | tf_op jit(solution)/shard_map/sum_scores/all_to_all | solution.py:305
  116.4 0.5 multiply_bitcast_fusion
  (8 shorter events, 0.0 us)
Async XLA Ops:
  1.9 1.1 copy-start
  3.0 1.0 copy-start.1
  4.1 1.0 copy-start.2
  5.1 1.0 copy-start.3
  6.2 0.9 copy-start.4
  7.1 0.7 copy-start.5
  8.6 36.9 %copy-start.7 = (bf16[2048,64]{0,1:T(8,128)(2,1)S(1)}, bf16[2048,64]{0,1:T(8,128)(2,1)}, u32[]{:S(2)}) copy-start(bf16[2048,64]{0,1:T(8,128)(2,1)} %param.18) | copy-start | bytes 786436
  38.7 7.1 %copy-start.8 = (bf16[512,64]{0,1:T(8,128)(2,1)S(1)}, bf16[512,64]{0,1:T(8,128)(2,1)}, u32[]{:S(2)}) copy-start(bf16[512,64]{0,1:T(8,128)(2,1)} %param.19) | copy-start | bytes 196612
  38.7 7.2 %copy-start.9 = (bf16[512,64]{0,1:T(8,128)(2,1)S(1)}, bf16[512,64]{0,1:T(8,128)(2,1)}, u32[]{:S(2)}) copy-start(bf16[512,64]{0,1:T(8,128)(2,1)} %param.20) | copy-start | bytes 196612
  39.7 7.9 %collective-permute-start = (bf16[8,128,384]{2,1,0:T(8,128)(2,1)}, bf16[8,128,384]{2,1,0:T(8,128)(2,1)S(1)}, u32[]{:S(2)}, u32[]{:S(2)}) collective-permute-start(bf16[8,128,384]{2,1,0:T(8,128)(2,1)} %slice.8), channel_id=1, source_target_pairs={{0,1},{1,0},{2,3},{3,2},{4,5},{5,4},{6,7},{7,6},{8,9},{9,8},{10,11... | collective-permute-start | bytes 2359304 | tf_op jit(solution)/shard_map/swap_cores/ppermute | solution.py:254
  46.1 12.3 %copy-start.6 = (s32[2]{0:T(128)}, s32[2]{0:T(128)S(1)}, u32[]{:S(2)}) copy-start(s32[2]{0:T(128)S(1)} %pad_add_fusion.at_ref) | copy-start | bytes 28
  105.8 10.5 %all-to-all-start.3 = ((f32[8,1,128]{2,1,0:T(1,128)}), f32[8,1,128]{2,1,0:T(1,128)S(1)}, u32[]{:S(2)}, u32[]{:S(2)}) async-start(f32[8,1,128]{2,1,0:T(1,128)} %score.1), calls=%async_computation.3 | async-start | bytes 8192 | tf_op jit(solution)/shard_map/sum_scores/all_to_all | solution.py:305

commit v2 on v1

v2 whole, which is shorter than its diff:
```python
import functools
import math

import jax
import jax.numpy as jnp
from jax import lax
from jax.experimental import pallas as pl
from jax.experimental.pallas import tpu as pltpu
from jax.sharding import PartitionSpec as P

KV_HEADS = 4
HEAD_DIM = 128
RANK = 64
LANES = 128
SCALE = HEAD_DIM ** (-0.5)
F32 = jnp.float32
BF16 = jnp.bfloat16
VMEM = pl.BlockSpec(memory_space=pltpu.VMEM)
SMEM = pl.BlockSpec(memory_space=pltpu.SMEM)

HBM = pl.BlockSpec(memory_space=pltpu.HBM)

Q_AT, D_AT, K_AT, V_AT, X_AT, WIDE = 0, 256, 512, 640, 768, 896


def nt(a, b):
    return lax.dot_general(a, b, (((1,), (1,)), ((), ())), preferred_element_type=F32)


def tn(a, b):
    return lax.dot_general(a, b, (((0,), (0,)), ((), ())), preferred_element_type=F32)


def nn(a, b):
    return jnp.dot(a, b, preferred_element_type=F32)


def split2(a):
    high = a.astype(BF16)
    return high, (a - high.astype(F32)).astype(BF16)


def lane_of(shape):
    return lax.broadcasted_iota(jnp.int32, shape, len(shape) - 1)


def row_of(shape):
    return lax.broadcasted_iota(jnp.int32, shape, len(shape) - 2)


def start_all(pairs, sems):
    copies = [pltpu.make_async_copy(src, dst, sems.at[i]) for i, (src, dst) in enumerate(pairs)]
    for copy in copies:
        copy.start()
    return copies


def row_parts(src, dst, parts):
    rows = src.shape[0] // parts
    return [(src.at[pl.ds(i * rows, rows)], dst.at[pl.ds(i * rows, rows)]) for i in range(parts)]


def message_kernel(
    h_hbm, q_hbm, kv_hbm, o_hbm, d_hbm, lse_hbm, pin_hbm, msg_ref, h_ref, kv_ref, o_ref, d_ref, lse_ref, pin_ref, sems
):
    tok = kv_ref.shape[0]
    heads = lse_ref.shape[0]
    chips = heads // 2
    group = heads // KV_HEADS
    two = 2 * HEAD_DIM
    parts = 2
    todo = [(lse_hbm, lse_ref)] + row_parts(d_hbm, d_ref, parts) + row_parts(o_hbm, o_ref, parts)
    deltas = len(todo)
    todo += [(pin_hbm, pin_ref)] + row_parts(h_hbm, h_ref, parts) + row_parts(kv_hbm, kv_ref, parts)
    inputs = len(todo)
    todo += [(q_hbm.at[:, pl.ds(p * two, two)], msg_ref.at[p, :, pl.ds(Q_AT, two)]) for p in range(chips)]
    copies = start_all(todo, sems)
    src = row_of((LANES, chips * LANES))
    dst = lane_of((LANES, chips * LANES))
    head = src % heads
    place = (head // 2) * LANES + RANK + (src // heads) * 6 + (head % 2) * 3
    place = jnp.where(src < 2 * heads, place, -8)
    picks = [jnp.where(dst == place + j, 1.0, 0.0).astype(BF16) for j in range(3)]
    for copy in copies[:deltas]:
        copy.wait()
    lse = jnp.concatenate([lse_ref[...], jnp.zeros((LANES - heads, tok), F32)], axis=0)
    terms = lse.T * (-1.0 / SCALE)
    lane = lane_of((tok, LANES))
    for h in range(heads):
        cols = slice(h * HEAD_DIM, (h + 1) * HEAD_DIM)
        prod = d_ref[:, cols].astype(F32) * o_ref[:, cols].astype(F32)
        delta = jnp.sum(prod, axis=1, keepdims=True)
        terms = jnp.where(lane == heads + h, -delta, terms)
    high = terms.astype(BF16)
    rest = terms - high.astype(F32)
    mid = rest.astype(BF16)
    low = (rest - mid.astype(F32)).astype(BF16)
    spread = nn(high, picks[0]) + nn(mid, picks[1]) + nn(low, picks[2])
    for p in range(chips):
        msg_ref[p, :, D_AT:K_AT] = d_ref[:, p * two : (p + 1) * two]
    for copy in copies[deltas:inputs]:
        copy.wait()
    x = nt(h_ref[...], pin_ref[...])
    x = jnp.concatenate([x, jnp.zeros((tok, LANES - RANK), F32)], axis=1)
    kv_cols = KV_HEADS * HEAD_DIM
    for p in range(chips):
        kv = 2 * p // group
        msg_ref[p, :, K_AT:V_AT] = kv_ref[:, kv * HEAD_DIM : (kv + 1) * HEAD_DIM]
        msg_ref[p, :, V_AT:X_AT] = kv_ref[:, kv_cols + kv * HEAD_DIM : kv_cols + (kv + 1) * HEAD_DIM]
        block = x + spread[:, p * LANES : (p + 1) * LANES]
        msg_ref[p, :, X_AT:] = block.astype(BF16)
    for copy in copies[inputs:]:
        copy.wait()


def message_call(hidden_in, queries, keys_values, attn_out, out_grad, log_norms, proj_in_t):
    tok = queries.shape[0]
    chips = log_norms.shape[0] // 2
    return pl.pallas_call(
        message_kernel,
        out_shape=jax.ShapeDtypeStruct((chips, tok, WIDE), BF16),
        in_specs=[HBM] * 7,
        out_specs=VMEM,
        scratch_shapes=[
            pltpu.VMEM(a.shape, a.dtype)
            for a in (hidden_in, keys_values, attn_out, out_grad, log_norms, proj_in_t)
        ]
        + [pltpu.SemaphoreType.DMA((2 + 4 * 2 + chips,))],
        compiler_params=pltpu.CompilerParams(vmem_limit_bytes=60 * 2**20),
    )(hidden_in, queries, keys_values, attn_out, out_grad, log_norms, proj_in_t)


def attention_kernel(
    at_ref, r_ref, o_ref, pq_ref, pk_ref, pv_ref, out_ref, qs, ds, qp, dp_, kt, vt, w, xk, ps, dss, rq, rk, rv,
):
    chip = at_ref[0]
    core = at_ref[1]
    blocks, tok, _ = r_ref.shape
    rows = blocks * tok
    half = 2 * tok
    groups = rows // half
    group = pk_ref.shape[1] // HEAD_DIM
    heads = pq_ref.shape[1] // HEAD_DIM
    per_kv = heads // group

    def part(ref, at):
        return ref[:, :, at : at + LANES].reshape(rows, LANES)

    lane = lane_of((rows, LANES))
    xl = part(r_ref, X_AT)
    none = jnp.zeros_like(xl)
    kv = (2 * chip) // per_kv
    kv_at = pl.ds(pl.multiple_of(kv * HEAD_DIM, HEAD_DIM), HEAD_DIM)
    pk = jnp.concatenate([pk_ref[:, kv_at]] * 2, axis=0)
    pv = jnp.concatenate([pv_ref[:, kv_at]] * 2, axis=0)
    first = lane < RANK

    def doubled(a, proj):
        full = nt(a, proj)
        high = full.astype(BF16).astype(F32)
        return jnp.where(first, high, full - high).astype(BF16)

    for h in range(2):
        q = part(r_ref, Q_AT + h * LANES)
        d = part(r_ref, D_AT + h * LANES)
        for ref, val, kind in ((qs, q, 0), (ds, d, 1)):
            start = RANK + kind * 6 + h * 3
            mask = (lane >= start) & (lane < start + 3)
            side = jnp.where(mask, xl, none)
            for g in range(groups):
                ref[g, h * half : (h + 1) * half, :LANES] = val[g * half : (g + 1) * half]
                ref[g, h * half : (h + 1) * half, LANES:] = side[g * half : (g + 1) * half]
        qp[h * rows : (h + 1) * rows] = doubled(q, pk)
        dp_[h * rows : (h + 1) * rows] = doubled(d, pv)

    kt[:, LANES:, :] = jnp.ones((2, LANES, rows), BF16)
    vt[:, LANES:, :] = jnp.ones((2, LANES, rows), BF16)
    for i, (src, base) in enumerate(((r_ref, 0), (o_ref, K_AT))):
        key = part(src, K_AT - base)
        kt[i, :LANES, :] = key.T
        vt[i, :LANES, :] = part(src, V_AT - base).T
        xk[i] = part(src, X_AT - base)
        for h in range(2):
            at = pl.multiple_of((2 * chip + h) * HEAD_DIM, HEAD_DIM)
            pq = pq_ref[:, pl.ds(at, HEAD_DIM)]
            w[h, i, :, :LANES] = doubled(key, jnp.concatenate([pq, pq], axis=0))
            w[h, i, :, LANES:] = xk[i]

    RB = 256
    fold = SCALE * math.log2(math.e)
    r_io = row_of((RB, half))
    c_io = lane_of((RB, half))
    for g in range(groups):
        upto = (g + 1) * half
        for i in range(2):
            for n in range(g + 1):
                cols = slice(n * half, (n + 1) * half)
                for r0 in range(0, 2 * half, RB):
                    rr = slice(r0, r0 + RB)
                    s = nn(qs[g, rr], kt[i, :, cols])
                    probs = jnp.exp2(s * fold)
                    if n == g:
                        ri = (r_io + r0) % half
                        if i == 0:
                            seen = c_io <= ri
                        else:
                            seen = (c_io // tok) < (ri // tok) + core
                        probs = jnp.where(seen, probs, 0.0)
                    dscores = probs * nn(ds[g, rr], vt[i, :, cols])
                    ps[i, rr, cols] = probs.astype(BF16)
                    dss[i, rr, cols] = dscores.astype(BF16)
        acc_v = nn(ps[0, :, :upto], xk[0, :upto]) + nn(ps[1, :, :upto], xk[1, :upto])
        vh, vl = split2(acc_v)
        sum_q = None
        for h in range(2):
            mine = slice(h * half, (h + 1) * half)
            to = slice(h * rows + g * half, h * rows + (g + 1) * half)
            acc = nn(dss[0, mine, :upto], w[h, 0, :upto]) + nn(dss[1, mine, :upto], w[h, 1, :upto])
            rv[to, :LANES] = vh[mine]
            rv[to, LANES:] = vl[mine]
            high, low = split2(acc[:, LANES:])
            rk[to, :LANES] = high
            rk[to, LANES:] = low
            sum_q = acc[:, :LANES] if h == 0 else sum_q + acc[:, :LANES]
        high, low = split2(sum_q)
        rq[g * half : (g + 1) * half, :LANES] = high
        rq[g * half : (g + 1) * half, LANES:] = low
    gq = tn(xl, rq[...])
    gk = tn(qp[...], rk[...])
    gv = tn(dp_[...], rv[...])

    def halves(a):
        return a[:, :LANES] + a[:, LANES:]

    tq = halves(gq[:RANK, :])
    out_q = (tq + pltpu.roll(tq, RANK, 1)) * SCALE
    tk = halves(gk[:RANK, :] + gk[RANK:, :])
    tv = halves(gv[:RANK, :] + gv[RANK:, :])
    zero = jnp.zeros((RANK, LANES), F32)
    tk = jnp.concatenate([tk, zero], axis=0).T[:RANK] * SCALE
    tv = jnp.concatenate([tv, zero], axis=0).T[:RANK]
    low_lanes = lane_of((RANK, LANES)) < RANK
    top = jnp.where(low_lanes, out_q, pltpu.roll(tk, RANK, 1))
    bottom = jnp.where(
        lane_of((RANK // 2, LANES)) < RANK, tv[: RANK // 2], pltpu.roll(tv, RANK, 1)[RANK // 2 :]
    )
    packed = jnp.concatenate([top, bottom], axis=0).astype(BF16)
    for i in range(out_ref.shape[0]):
        out_ref[i] = packed


def attention_call(at, got, other, proj_q, proj_k, proj_v):
    chips, tok, _ = got.shape
    rows = chips * tok
    half = 2 * tok
    groups = rows // half
    return pl.pallas_call(
        attention_kernel,
        out_shape=jax.ShapeDtypeStruct((2 * chips, 3 * RANK // 2, LANES), BF16),
        in_specs=[SMEM] + [VMEM] * 5,
        out_specs=VMEM,
        scratch_shapes=[
            pltpu.VMEM((groups, 2 * half, 2 * LANES), BF16),
            pltpu.VMEM((groups, 2 * half, 2 * LANES), BF16),
            pltpu.VMEM((2 * rows, LANES), BF16),
            pltpu.VMEM((2 * rows, LANES), BF16),
            pltpu.VMEM((2, 2 * LANES, rows), BF16),
            pltpu.VMEM((2, 2 * LANES, rows), BF16),
            pltpu.VMEM((2, 2, rows, 2 * LANES), BF16),
            pltpu.VMEM((2, rows, LANES), BF16),
            pltpu.VMEM((2, 2 * half, rows), BF16),
            pltpu.VMEM((2, 2 * half, rows), BF16),
            pltpu.VMEM((rows, 2 * LANES), BF16),
            pltpu.VMEM((2 * rows, 2 * LANES), BF16),
            pltpu.VMEM((2 * rows, 2 * LANES), BF16),
        ],
        compiler_params=pltpu.CompilerParams(vmem_limit_bytes=40 * 2**20),
    )(at, got, other, proj_q, proj_k, proj_v)


def unit_kernel(at_ref, parts_ref, unit_ref, mine_ref, send_ref, flat):
    total = parts_ref[0].astype(F32)
    for i in range(1, parts_ref.shape[0]):
        total = total + parts_ref[i].astype(F32)
    mean = jnp.sum(jnp.sum(total * total, axis=0, keepdims=True), axis=1, keepdims=True) / (3.0 * RANK * RANK)
    unit = total / jnp.sqrt(mean + 1e-6)
    unit_ref[:, :LANES] = unit[:RANK]
    unit_ref[: RANK // 2, LANES:] = unit[RANK:, :RANK]
    unit_ref[RANK // 2 :, LANES:] = unit[RANK:, RANK:]
    flat[: unit.shape[0], :] = unit
    flat[unit.shape[0] :, :] = jnp.zeros((flat.shape[0] - unit.shape[0], LANES), F32)
    depth = mine_ref.shape[0]
    mine = flat[pl.ds(pl.multiple_of(at_ref[0] * depth, depth), depth), :]
    mine_ref[...] = mine
    send = mine.astype(BF16)
    for i in range(send_ref.shape[0]):
        send_ref[i] = send


def score_kernel(docs_ref, mine_ref, every_ref, out_ref):
    mine = mine_ref[...]
    terms = []
    for q in range(docs_ref.shape[0]):
        other = every_ref[docs_ref[q]].astype(F32)
        terms.append(jnp.sum(mine * other, axis=0, keepdims=True))
    terms = jnp.concatenate(terms, axis=0)
    for i in range(out_ref.shape[0]):
        out_ref[i] = terms


def local(
    hidden_in, queries, keys_values, attn_out, out_grad, log_norms, proj_in, proj_q, proj_k, proj_v, query_docs
):
    tok = queries.shape[1]
    heads = log_norms.shape[1]
    chips = heads // 2
    docs = lax.axis_size("dp")
    count = query_docs.shape[0]
    same_core = [[2 * p + c for p in range(chips)] for c in range(2)]
    index = lax.axis_index("ctx")
    at = jnp.stack([lax.shift_right_logical(index, 1), index & 1])

    with jax.named_scope("message"):
        msg = message_call(
            hidden_in[0], queries[0], keys_values[0], attn_out[0], out_grad[0], log_norms[0], proj_in.T
        )
    with jax.named_scope("exchange_heads"):
        got = lax.all_to_all(msg, "ctx", 0, 0, axis_index_groups=same_core, tiled=True)
    with jax.named_scope("swap_cores"):
        other = lax.ppermute(got[:, :, K_AT:], "ctx", [(i, i ^ 1) for i in range(2 * chips)])
    with jax.named_scope("attention"):
        partial = attention_call(at, got, other, proj_q.T, proj_k.T, proj_v.T)
    with jax.named_scope("sum_parts"):
        parts = lax.all_to_all(partial, "ctx", 0, 0, tiled=True)
    with jax.named_scope("unit"):
        unit, mine, send = pl.pallas_call(
            unit_kernel,
            out_shape=(
                jax.ShapeDtypeStruct((RANK, 3 * RANK), F32),
                jax.ShapeDtypeStruct((16, LANES), F32),
                jax.ShapeDtypeStruct((docs, 16, LANES), BF16),
            ),
            in_specs=[SMEM, VMEM],
            out_specs=(VMEM, VMEM, VMEM),
            scratch_shapes=[pltpu.VMEM((16 * chips, LANES), F32)],
            compiler_params=pltpu.CompilerParams(vmem_limit_bytes=8 * 2**20),
        )(at, parts)
    with jax.named_scope("exchange_documents"):
        every = lax.all_to_all(send, "dp", 0, 0, tiled=True)
    with jax.named_scope("score"):
        terms = pl.pallas_call(
            score_kernel,
            out_shape=jax.ShapeDtypeStruct((chips, count, LANES), F32),
            in_specs=[SMEM, VMEM, VMEM],
            out_specs=VMEM,
            compiler_params=pltpu.CompilerParams(vmem_limit_bytes=8 * 2**20),
        )(query_docs, mine, every)
    with jax.named_scope("sum_scores"):
        terms = lax.all_to_all(terms, "ctx", 0, 0, axis_index_groups=same_core, tiled=True)
    scores = jnp.sum(terms, axis=(0, 2))[None] / (3.0 * RANK * RANK)
    return (unit.reshape(1, -1), scores)


def solution(mesh):
    in_specs = (
        P("dp", "ctx", None),
        P("dp", "ctx", None),
        P("dp", "ctx", None),
        P("dp", "ctx", None),
        P("dp", "ctx", None),
        P("dp", None, "ctx"),
        P(),
        P(),
        P(),
        P(),
        P(),
    )
    out_specs = (P("dp", None), P("dp", None))
    return jax.shard_map(local, mesh=mesh, in_specs=in_specs, out_specs=out_specs, check_vma=False)
```

time: 119 us -> 110 us (0.924)
  local copies, waits for them, and re-layouts: 10.2 us -> 1.74 us
  blocking collectives: 73.9 us -> 72.3 us
  waiting for transfers between devices: 6.38 us -> 7.91 us
    unnamed x24 -> x8, local copies, waits for them, and re-layouts: 7.67 us -> 0.02 us
  transfers between devices with their start and end apart: 2 -> 2, of which waited for: 2 -> 2; matrix products, arithmetic and copies ran while one was open for 2% -> 1% of each run, Pallas kernels for 0% -> 0%
where the time goes in v2:
time: 110 us; the launch traced here: 108 us
  blocking collectives  72.3 us (66%)
  Pallas kernels  14.1 us (13%)
  starting transfers between devices  10.6 us (10%)
  waiting for transfers between devices  7.91 us (7%)
  local copies, waits for them, and re-layouts  1.74 us (2%)
    all_to_all x1, blocking collectives, local(): every = lax.all_to_all(send, 'dp', 0, 0, tiled=True)  30 us
    all_to_all x1, blocking collectives, local(): lax.all_to_all(msg, 'ctx', 0, 0, axis_index_groups=same_core, tiled=True)  29.4 us
    all_to_all x1, blocking collectives, local(): parts = lax.all_to_all(partial, 'ctx', 0, 0, tiled=True)  12.9 us
    pallas_call x1, Pallas kernels, attention_call(): pl.pallas_call(attention_kernel, out_shape=jax.ShapeDtypeStruct((2 * chip...  8.09 us
    ppermute x1, starting transfers between devices, local(): lax.ppermute(got[:, :, K_AT:], 'ctx', [(i, i ^ 1) for i in range(2 * chip...  6.66 us
    all_to_all x1, waiting for transfers between devices, local(): lax.all_to_all(terms, 'ctx', 0, 0, axis_index_groups=same_core, tiled=True)  5.89 us
    pallas_call x1, Pallas kernels, message_call(): pl.pallas_call(message_kernel, out_shape=jax.ShapeDtypeStruct((chips, tok...  4.06 us
    all_to_all x1, starting transfers between devices, local(): lax.all_to_all(terms, 'ctx', 0, 0, axis_index_groups=same_core, tiled=True)  3.98 us
  transfers between devices with their start and end apart: 2, of which 2 were waited for; matrix products, arithmetic and copies ran while one was open for 1% of the time, Pallas kernels for 0%

profile of v2, /device:TPU:1, one launch (start us, length us, event | category | flops | bytes accessed | tf_op | source)
XLA Modules:
  0.0 108.0 jit_solution(13197766059638333391)
XLA Ops:
  0.6 4.1 %message.1 = bf16[8,128,896]{2,1,0:T(8,128)(2,1)} custom-call(bf16[128,2560]{1,0:T(8,128)(2,1)} %bitcast.17, bf16[128,2048]{1,0:T(8,128)(2,1)} %bitcast.18, bf16[128,1024]{1,0:T(8,128)(2,1)} %bitcast.22, bf16[128,2048]{1,0:T(8,128)(2,1)} %bitcast.19, bf16[128,2048]{1,0:T(8,128)(2,1)} %bitcast.20, f32[16,128]{1,0:T(8,128)} %bitcast.23, bf16[64,2560]{1,0:T(8,128)(2,1)} %bitcast.21), custom_call_target="tpu_custom_call" | custom-call | tf_op jit(solution)/shard_map/message/pallas_call | solution.py:119
  4.7 0.0 copy-start
  4.7 0.0 copy-start.1
  4.7 0.0 copy-start.2
  4.7 29.4 %all_to_all.20.r_ref = bf16[8,128,896]{2,1,0:T(8,128)(2,1)S(1)} all-to-all(bf16[8,128,896]{2,1,0:T(8,128)(2,1)} %message.1), channel_id=1, replica_groups={{0,2,4,6,8,10,12,14},{1,3,5,7,9,11,13,15},{16,18,20,22,24,26,28,30},{17..., dimensions={0} | all-to-all | bytes 3670016 | tf_op jit(solution)/shard_map/exchange_heads/all_to_all | solution.py:328
  34.1 1.0 slice.4
  35.1 6.7 %collective-permute-start = (bf16[8,128,384]{2,1,0:T(8,128)(2,1)}, bf16[8,128,384]{2,1,0:T(8,128)(2,1)S(1)}, u32[]{:S(2)}, u32[]{:S(2)}) collective-permute-start(bf16[8,128,384]{2,1,0:T(8,128)(2,1)} %slice.4), channel_id=1, source_target_pairs={{0,1},{1,0},{2,3},{3,2},{4,5},{5,4},{6,7},{7,6},{8,9},{9,8},{10,11... | collective-permute-start | bytes 2359304 | tf_op jit(solution)/shard_map/swap_cores/ppermute | solution.py:330
  41.8 0.1 pad_add_fusion.at_ref
  41.9 2.0 %collective-permute-done.o_ref = bf16[8,128,384]{2,1,0:T(8,128)(2,1)S(1)} collective-permute-done((bf16[8,128,384]{2,1,0:T(8,128)(2,1)}, bf16[8,128,384]{2,1,0:T(8,128)(2,1)S(1)}, u32[]{:S(2)}, u32[]{:S(2)}) %collective-permute-start) | collective-permute-done | bytes 786464 | tf_op jit(solution)/shard_map/swap_cores/ppermute | solution.py:330
  43.9 0.0 copy-done
  43.9 0.0 copy-done.1
  43.9 0.0 copy-done.2
  43.9 0.0 copy-start.3
  43.9 8.1 %attention.1 = bf16[16,96,128]{2,1,0:T(8,128)(2,1)S(1)} custom-call(s32[2]{0:T(128)S(1)} %pad_add_fusion.at_ref, bf16[8,128,896]{2,1,0:T(8,128)(2,1)S(1)} %all_to_all.20.r_ref, bf16[8,128,384]{2,1,0:T(8,128)(2,1)S(1)} %collective-permute-done.o_ref, bf16[64,2048]{1,0:T(8,128)(2,1)S(1)} %bitcast.14, bf16[64,512]{1,0:T(8,128)(2,1)S(1)} %bitcast.15, ...), custom_call_target="tpu_custom_call" | custom-call | tf_op jit(solution)/shard_map/attention/pallas_call | solution.py:257
  52.0 12.9 %all_to_all.21.parts_ref = bf16[16,96,128]{2,1,0:T(8,128)(2,1)S(1)} all-to-all(bf16[16,96,128]{2,1,0:T(8,128)(2,1)S(1)} %attention.1), channel_id=1, replica_groups=mesh['dp'=32,'ctx'=16] {'ctx'}, dimensions={0} | all-to-all | bytes 786432 | tf_op jit(solution)/shard_map/sum_parts/all_to_all | solution.py:334
  64.9 0.8 unit.1
  65.6 30.0 %all_to_all.22.every_ref = bf16[32,16,128]{2,1,0:T(8,128)(2,1)S(1)} all-to-all(bf16[32,16,128]{2,1,0:T(8,128)(2,1)S(1)} %get-tuple-element.7), channel_id=1, replica_groups=mesh['dp'=32,'ctx'=16] {'dp'}, dimensions={0} | all-to-all | bytes 262144 | tf_op jit(solution)/shard_map/exchange_documents/all_to_all | solution.py:349
  95.6 0.0 copy-done.3
  95.6 1.2 %score.1 = f32[8,8,128]{2,1,0:T(8,128)} custom-call(s32[8]{0:T(128)S(1)} %copy-done.3, f32[16,128]{1,0:T(8,128)S(1)} %get-tuple-element.6.mine_ref, bf16[32,16,128]{2,1,0:T(8,128)(2,1)S(1)} %all_to_all.22.every_ref), custom_call_target="tpu_custom_call" | custom-call | tf_op jit(solution)/shard_map/score/pallas_call | solution.py:351
  96.8 4.0 %all-to-all-start.3 = ((f32[8,8,128]{2,1,0:T(8,128)}), f32[8,8,128]{2,1,0:T(8,128)S(1)}, u32[]{:S(2)}, u32[]{:S(2)}) async-start(f32[8,8,128]{2,1,0:T(8,128)} %score.1), calls=%async_computation.3 | async-start | bytes 65536 | tf_op jit(solution)/shard_map/sum_scores/all_to_all | solution.py:359
  100.8 0.7 reshape.17
  101.5 5.9 %all-to-all-done.3 = f32[8,8,128]{2,1,0:T(8,128)S(1)} async-done(((f32[8,8,128]{2,1,0:T(8,128)}), f32[8,8,128]{2,1,0:T(8,128)S(1)}, u32[]{:S(2)}, u32[]{:S(2)}) %all-to-all-start.3) | async-done | bytes 32800 | tf_op jit(solution)/shard_map/sum_scores/all_to_all | solution.py:359
  107.4 0.1 reduce_sum.9
  107.5 0.5 multiply_bitcast_fusion
Async XLA Ops:
  4.7 39.2 %copy-start = (bf16[2048,64]{0,1:T(8,128)(2,1)S(1)}, bf16[2048,64]{0,1:T(8,128)(2,1)}, u32[]{:S(2)}) copy-start(bf16[2048,64]{0,1:T(8,128)(2,1)} %param.18) | copy-start | bytes 786436
  4.7 39.2 %copy-start.1 = (bf16[512,64]{0,1:T(8,128)(2,1)S(1)}, bf16[512,64]{0,1:T(8,128)(2,1)}, u32[]{:S(2)}) copy-start(bf16[512,64]{0,1:T(8,128)(2,1)} %param.19) | copy-start | bytes 196612
  4.7 39.2 %copy-start.2 = (bf16[512,64]{0,1:T(8,128)(2,1)S(1)}, bf16[512,64]{0,1:T(8,128)(2,1)}, u32[]{:S(2)}) copy-start(bf16[512,64]{0,1:T(8,128)(2,1)} %param.20) | copy-start | bytes 196612
  35.1 8.8 %collective-permute-start = (bf16[8,128,384]{2,1,0:T(8,128)(2,1)}, bf16[8,128,384]{2,1,0:T(8,128)(2,1)S(1)}, u32[]{:S(2)}, u32[]{:S(2)}) collective-permute-start(bf16[8,128,384]{2,1,0:T(8,128)(2,1)} %slice.4), channel_id=1, source_target_pairs={{0,1},{1,0},{2,3},{3,2},{4,5},{5,4},{6,7},{7,6},{8,9},{9,8},{10,11... | collective-permute-start | bytes 2359304 | tf_op jit(solution)/shard_map/swap_cores/ppermute | solution.py:330
  43.9 51.7 %copy-start.3 = (s32[8]{0:T(128)S(1)}, s32[8]{0:T(128)}, u32[]{:S(2)}) copy-start(s32[8]{0:T(128)} %docs_ref.1) | copy-start | bytes 100
  96.8 10.6 %all-to-all-start.3 = ((f32[8,8,128]{2,1,0:T(8,128)}), f32[8,8,128]{2,1,0:T(8,128)S(1)}, u32[]{:S(2)}, u32[]{:S(2)}) async-start(f32[8,8,128]{2,1,0:T(8,128)} %score.1), calls=%async_computation.3 | async-start | bytes 65536 | tf_op jit(solution)/shard_map/sum_scores/all_to_all | solution.py:359

commit v3 on v2

v3 whole, which is shorter than its diff:
```python
import functools
import math

import jax
import jax.numpy as jnp
from jax import lax
from jax.experimental import pallas as pl
from jax.experimental.pallas import tpu as pltpu
from jax.sharding import PartitionSpec as P

KV_HEADS = 4
HEAD_DIM = 128
RANK = 64
LANES = 128
SCALE = HEAD_DIM ** (-0.5)
F32 = jnp.float32
BF16 = jnp.bfloat16
VMEM = pl.BlockSpec(memory_space=pltpu.VMEM)
SMEM = pl.BlockSpec(memory_space=pltpu.SMEM)

HBM = pl.BlockSpec(memory_space=pltpu.HBM)

Q_AT, D_AT, V_AT, K_AT, X_AT, WIDE = 0, 256, 512, 640, 768, 896


def nt(a, b):
    return lax.dot_general(a, b, (((1,), (1,)), ((), ())), preferred_element_type=F32)


def tn(a, b):
    return lax.dot_general(a, b, (((0,), (0,)), ((), ())), preferred_element_type=F32)


def nn(a, b):
    return jnp.dot(a, b, preferred_element_type=F32)


def split2(a):
    high = a.astype(BF16)
    return high, (a - high.astype(F32)).astype(BF16)


def lane_of(shape):
    return lax.broadcasted_iota(jnp.int32, shape, len(shape) - 1)


def row_of(shape):
    return lax.broadcasted_iota(jnp.int32, shape, len(shape) - 2)


def place():
    index = lax.axis_index("ctx")
    return lax.div(index, 2), lax.rem(index, 2)


def start_all(pairs, sems):
    copies = [pltpu.make_async_copy(src, dst, sems.at[i]) for i, (src, dst) in enumerate(pairs)]
    for copy in copies:
        copy.start()
    return copies


def row_parts(src, dst, parts):
    rows = src.shape[0] // parts
    return [(src.at[pl.ds(i * rows, rows)], dst.at[pl.ds(i * rows, rows)]) for i in range(parts)]


def message_kernel(
    h_hbm, q_hbm, kv_hbm, o_hbm, d_hbm, lse_hbm, pin_hbm, pq_hbm, pk_hbm, pv_hbm, msg_ref, proj_ref,
    h_ref, kv_ref, o_ref, d_ref, lse_ref, pin_ref, sems,
):
    tok = kv_ref.shape[0]
    heads = lse_ref.shape[0]
    chips = heads // 2
    group = heads // KV_HEADS
    two = 2 * HEAD_DIM
    parts = 2
    chip, _ = place()
    kv_at = head_at(lax.div(2 * chip, group))
    pairs = pl.ds(pl.multiple_of(chip * two, two), two)
    todo = [(pq_hbm.at[:, pairs], proj_ref.at[:, pl.ds(0, two)])]
    todo += [(pk_hbm.at[:, kv_at], proj_ref.at[:, pl.ds(two, HEAD_DIM)])]
    todo += [(pv_hbm.at[:, kv_at], proj_ref.at[:, pl.ds(two + HEAD_DIM, HEAD_DIM)])]
    todo += [(lse_hbm, lse_ref)] + row_parts(d_hbm, d_ref, parts) + row_parts(o_hbm, o_ref, parts)
    deltas = len(todo)
    todo += [(pin_hbm, pin_ref)] + row_parts(h_hbm, h_ref, parts) + row_parts(kv_hbm, kv_ref, parts)
    inputs = len(todo)
    todo += [(q_hbm.at[:, pl.ds(p * two, two)], msg_ref.at[p, :, pl.ds(Q_AT, two)]) for p in range(chips)]
    copies = start_all(todo, sems)
    src = row_of((LANES, chips * LANES))
    dst = lane_of((LANES, chips * LANES))
    head = src % heads
    to = (head // 2) * LANES + RANK + (src // heads) * 6 + (head % 2) * 3
    to = jnp.where(src < 2 * heads, to, -8)
    picks = [jnp.where(dst == to + j, 1.0, 0.0).astype(BF16) for j in range(3)]
    for copy in copies[:deltas]:
        copy.wait()
    lse = jnp.concatenate([lse_ref[...], jnp.zeros((LANES - heads, tok), F32)], axis=0)
    terms = lse.T * (-1.0 / SCALE)
    lane = lane_of((tok, LANES))
    for h in range(heads):
        cols = slice(h * HEAD_DIM, (h + 1) * HEAD_DIM)
        prod = d_ref[:, cols].astype(F32) * o_ref[:, cols].astype(F32)
        delta = jnp.sum(prod, axis=1, keepdims=True)
        terms = jnp.where(lane == heads + h, -delta, terms)
    high = terms.astype(BF16)
    rest = terms - high.astype(F32)
    mid = rest.astype(BF16)
    low = (rest - mid.astype(F32)).astype(BF16)
    spread = nn(high, picks[0]) + nn(mid, picks[1]) + nn(low, picks[2])
    for p in range(chips):
        msg_ref[p, :, D_AT:V_AT] = d_ref[:, p * two : (p + 1) * two]
    for copy in copies[deltas:inputs]:
        copy.wait()
    x = nt(h_ref[...], pin_ref[...])
    x = jnp.concatenate([x, jnp.zeros((tok, LANES - RANK), F32)], axis=1)
    kv_cols = KV_HEADS * HEAD_DIM
    for p in range(chips):
        kv = 2 * p // group
        msg_ref[p, :, V_AT:K_AT] = kv_ref[:, kv_cols + kv * HEAD_DIM : kv_cols + (kv + 1) * HEAD_DIM]
        msg_ref[p, :, K_AT:X_AT] = kv_ref[:, kv * HEAD_DIM : (kv + 1) * HEAD_DIM]
        block = x + spread[:, p * LANES : (p + 1) * LANES]
        msg_ref[p, :, X_AT:] = block.astype(BF16)
    for copy in copies[inputs:]:
        copy.wait()


def message_call(hidden_in, queries, keys_values, attn_out, out_grad, log_norms, proj_in_t, *proj_t):
    tok = queries.shape[0]
    chips = log_norms.shape[0] // 2
    return pl.pallas_call(
        message_kernel,
        out_shape=(
            jax.ShapeDtypeStruct((chips, tok, WIDE), BF16),
            jax.ShapeDtypeStruct((RANK, 4 * HEAD_DIM), BF16),
        ),
        in_specs=[HBM] * 10,
        out_specs=(VMEM, VMEM),
        scratch_shapes=[
            pltpu.VMEM(a.shape, a.dtype)
            for a in (hidden_in, keys_values, attn_out, out_grad, log_norms, proj_in_t)
        ]
        + [pltpu.SemaphoreType.DMA((13 + chips,))],
        compiler_params=pltpu.CompilerParams(vmem_limit_bytes=60 * 2**20),
    )(hidden_in, queries, keys_values, attn_out, out_grad, log_norms, proj_in_t, *proj_t)


def part(ref, at):
    return ref[:, :, at : at + LANES].reshape(ref.shape[0] * ref.shape[1], LANES)


def head_at(index):
    return pl.ds(pl.multiple_of(index * HEAD_DIM, HEAD_DIM), HEAD_DIM)


def load_keys(ref, base, kt, vt):
    rows = ref.shape[0] * ref.shape[1]
    for to, at in ((kt, K_AT), (vt, V_AT)):
        to[:LANES, :] = part(ref, at - base).T
        to[LANES:, :] = jnp.ones((LANES, rows), BF16)


def group_terms(g, tok, base, seen_of, qs, ds, keys_ref, kt, vt, ps, dss):
    half = 2 * tok
    upto = (g + 1) * half
    fold = SCALE * math.log2(math.e)
    for n in range(g + 1):
        cols = slice(n * half, (n + 1) * half)
        for h in range(2):
            rr = slice(h * half, (h + 1) * half)
            s = nn(qs[g, rr], kt[:, cols])
            probs = jnp.exp2(s * fold)
            if n == g:
                probs = jnp.where(seen_of(row_of((half, half)), lane_of((half, half))), probs, 0.0)
            dscores = probs * nn(ds[g, rr], vt[:, cols])
            ps[rr, cols] = probs.astype(BF16)
            dss[rr, cols] = dscores.astype(BF16)
    keys = keys_ref[: 2 * (g + 1), :, K_AT - base :].reshape(upto, 2 * LANES)
    return nn(ps[:, :upto], keys[:, LANES:]), nn(dss[:, :upto], keys)


def own_kernel(r_ref, qs, ds, acc, acc_v, kt, vt, ps, dss):
    blocks, tok, _ = r_ref.shape
    rows = blocks * tok
    half = 2 * tok
    groups = rows // half
    lane = lane_of((rows, LANES))
    xl = part(r_ref, X_AT)
    none = jnp.zeros_like(xl)
    load_keys(r_ref, 0, kt, vt)
    for h in range(2):
        for ref, at, kind in ((qs, Q_AT, 0), (ds, D_AT, 1)):
            val = part(r_ref, at + h * LANES)
            start = RANK + kind * 6 + h * 3
            side = jnp.where((lane >= start) & (lane < start + 3), xl, none)
            for g in range(groups):
                ref[g, h * half : (h + 1) * half, :LANES] = val[g * half : (g + 1) * half]
                ref[g, h * half : (h + 1) * half, LANES:] = side[g * half : (g + 1) * half]
    for g in range(groups):
        to = slice(2 * g * half, 2 * (g + 1) * half)
        acc_v[to], acc[to] = group_terms(g, tok, 0, lambda r, c: c <= r, qs, ds, r_ref, kt, vt, ps, dss)


def other_kernel(r_ref, o_ref, proj_ref, qs, ds, acc, acc_v, out_ref, kt, vt, ps, dss, rq, rk, rv):
    _, core = place()
    blocks, tok, _ = r_ref.shape
    rows = blocks * tok
    half = 2 * tok
    groups = rows // half
    load_keys(o_ref, V_AT, kt, vt)

    def seen_of(r, c):
        return (c // tok) < (r // tok) + core

    for g in range(groups):
        to = slice(2 * g * half, 2 * (g + 1) * half)
        for_v, for_qk = group_terms(g, tok, V_AT, seen_of, qs, ds, o_ref, kt, vt, ps, dss)
        for_v, for_qk = for_v + acc_v[to], for_qk + acc[to]
        for ref, val in ((rv, for_v), (rk, for_qk[:, LANES:]), (rq, for_qk[:, :LANES])):
            high, low = split2(val)
            for h in range(2):
                mine = slice(h * half, (h + 1) * half)
                at = slice(h * rows + g * half, h * rows + (g + 1) * half)
                ref[at, :LANES] = high[mine]
                ref[at, LANES:] = low[mine]

    def halves(a):
        return a[:, :LANES] + a[:, LANES:]

    def exact(a, b, product):
        high, low = split2(a)
        return product(high, b) + product(low, b)

    xl = part(r_ref, X_AT)
    zero = jnp.zeros((RANK, LANES), F32)
    out_q = zero
    mk = jnp.zeros((LANES, LANES), F32)
    mv = jnp.zeros((LANES, LANES), F32)
    for h in range(2):
        at = slice(h * rows, (h + 1) * rows)
        mq = halves(tn(xl, rq[at])[:RANK])
        pq = jnp.concatenate([proj_ref[:, h * HEAD_DIM : (h + 1) * HEAD_DIM], zero.astype(BF16)], axis=0)
        out_q = out_q + exact(mq, pq, nt)
        mk = mk + halves(tn(part(r_ref, Q_AT + h * LANES), rk[at]))
        mv = mv + halves(tn(part(r_ref, D_AT + h * LANES), rv[at]))
    mk_high, mk_low = split2(mk)
    mv_high, mv_low = split2(mv)
    pk = proj_ref[:, 2 * HEAD_DIM : 3 * HEAD_DIM]
    pv = proj_ref[:, 3 * HEAD_DIM :]
    tk = nn(pk, mk_high) + nn(pk, mk_low)
    tv = nn(pv, mv_high) + nn(pv, mv_low)
    tk = jnp.concatenate([tk, zero], axis=0).T[:RANK] * SCALE
    tv = jnp.concatenate([tv, zero], axis=0).T[:RANK]
    low_lanes = lane_of((RANK, LANES)) < RANK
    top = jnp.where(low_lanes, out_q * SCALE, pltpu.roll(tk, RANK, 1))
    bottom = jnp.where(low_lanes[: RANK // 2], tv[: RANK // 2], pltpu.roll(tv, RANK, 1)[RANK // 2 :])
    packed = jnp.concatenate([top, bottom], axis=0).astype(BF16)
    for i in range(out_ref.shape[0]):
        out_ref[i] = packed


def keys_kernel(r_ref, out_ref):
    out_ref[...] = r_ref[:, :, V_AT:]


def keys_call(got):
    chips, tok, _ = got.shape
    return pl.pallas_call(
        keys_kernel,
        out_shape=jax.ShapeDtypeStruct((chips, tok, WIDE - V_AT), BF16),
        in_specs=[VMEM],
        out_specs=VMEM,
        compiler_params=pltpu.CompilerParams(vmem_limit_bytes=8 * 2**20),
    )(got)


def attention_scratch(rows, half):
    return [
        pltpu.VMEM((2 * LANES, rows), BF16),
        pltpu.VMEM((2 * LANES, rows), BF16),
        pltpu.VMEM((2 * half, rows), BF16),
        pltpu.VMEM((2 * half, rows), BF16),
    ]


def own_call(got):
    chips, tok, _ = got.shape
    rows = chips * tok
    half = 2 * tok
    groups = rows // half
    return pl.pallas_call(
        own_kernel,
        out_shape=(
            jax.ShapeDtypeStruct((groups, 2 * half, 2 * LANES), BF16),
            jax.ShapeDtypeStruct((groups, 2 * half, 2 * LANES), BF16),
            jax.ShapeDtypeStruct((2 * rows, 2 * LANES), F32),
            jax.ShapeDtypeStruct((2 * rows, LANES), F32),
        ),
        in_specs=[VMEM],
        out_specs=(VMEM,) * 4,
        scratch_shapes=attention_scratch(rows, half),
        compiler_params=pltpu.CompilerParams(vmem_limit_bytes=24 * 2**20),
        cost_estimate=pl.CostEstimate(
            flops=2 * 4 * 2 * rows * rows * 2 * LANES, bytes_accessed=8 * 2**20, transcendentals=rows * rows
        ),
    )(got)


def other_call(got, other, proj, saved):
    chips, tok, _ = got.shape
    rows = chips * tok
    half = 2 * tok
    return pl.pallas_call(
        other_kernel,
        out_shape=jax.ShapeDtypeStruct((2 * chips, 3 * RANK // 2, LANES), BF16),
        in_specs=[VMEM] * 7,
        out_specs=VMEM,
        scratch_shapes=attention_scratch(rows, half) + [pltpu.VMEM((2 * rows, 2 * LANES), BF16)] * 3,
        compiler_params=pltpu.CompilerParams(vmem_limit_bytes=24 * 2**20),
    )(got, other, proj, *saved)


def attention_call(got, other, proj):
    return other_call(got, other, proj, own_call(got))


def unit_kernel(parts_ref, unit_ref, mine_ref, send_ref, flat):
    total = parts_ref[0].astype(F32)
    for i in range(1, parts_ref.shape[0]):
        total = total + parts_ref[i].astype(F32)
    mean = jnp.sum(jnp.sum(total * total, axis=0, keepdims=True), axis=1, keepdims=True) / (3.0 * RANK * RANK)
    unit = total / jnp.sqrt(mean + 1e-6)
    unit_ref[:, :LANES] = unit[:RANK]
    unit_ref[: RANK // 2, LANES:] = unit[RANK:, :RANK]
    unit_ref[RANK // 2 :, LANES:] = unit[RANK:, RANK:]
    flat[: unit.shape[0], :] = unit
    flat[unit.shape[0] :, :] = jnp.zeros((flat.shape[0] - unit.shape[0], LANES), F32)
    depth = mine_ref.shape[0]
    chip, _ = place()
    mine = flat[pl.ds(pl.multiple_of(chip * depth, depth), depth), :]
    mine_ref[...] = mine
    send = mine.astype(BF16)
    for i in range(send_ref.shape[0]):
        send_ref[i] = send


def split3(a):
    high, rest = split2(a)
    rest = a - high.astype(F32)
    mid, low = split2(rest)
    return high, mid, low


def score_kernel(docs_ref, mine_ref, every_ref, out_ref):
    mine = mine_ref[...]
    docs = every_ref.shape[0]
    terms = [jnp.sum(mine * every_ref[e].astype(F32), axis=0, keepdims=True) for e in range(docs)]
    terms = jnp.concatenate(terms, axis=0)
    ones = jnp.ones((8, LANES), BF16)
    sums = sum(nt(ones, t) for t in split3(terms))
    asked = docs_ref[...]
    picks = jnp.where(row_of((docs, asked.shape[1])) == asked, 1.0, 0.0).astype(BF16)
    picked = sum(nn(t, picks) for t in split3(sums))
    for i in range(out_ref.shape[0]):
        out_ref[i] = picked[:1]


def local(
    hidden_in, queries, keys_values, attn_out, out_grad, log_norms, proj_in, proj_q, proj_k, proj_v, query_docs
):
    tok = queries.shape[1]
    heads = log_norms.shape[1]
    chips = heads // 2
    docs = lax.axis_size("dp")
    count = query_docs.shape[0]
    same_core = [[2 * p + c for p in range(chips)] for c in range(2)]

    with jax.named_scope("message"):
        msg, proj = message_call(
            hidden_in[0], queries[0], keys_values[0], attn_out[0], out_grad[0], log_norms[0],
            proj_in.T, proj_q.T, proj_k.T, proj_v.T,
        )
    with jax.named_scope("exchange_heads"):
        got = lax.all_to_all(msg, "ctx", 0, 0, axis_index_groups=same_core, tiled=True)
    with jax.named_scope("swap_cores"):
        other = lax.ppermute(keys_call(got), "ctx", [(i, i ^ 1) for i in range(2 * chips)])
    with jax.named_scope("own_keys"):
        saved = own_call(got)
    with jax.named_scope("other_keys"):
        partial = other_call(got, other, proj, saved)
    with jax.named_scope("sum_parts"):
        parts = lax.all_to_all(partial, "ctx", 0, 0, tiled=True)
    with jax.named_scope("unit"):
        unit, mine, send = pl.pallas_call(
            unit_kernel,
            out_shape=(
                jax.ShapeDtypeStruct((RANK, 3 * RANK), F32),
                jax.ShapeDtypeStruct((16, LANES), F32),
                jax.ShapeDtypeStruct((docs, 16, LANES), BF16),
            ),
            in_specs=[VMEM],
            out_specs=(VMEM, VMEM, VMEM),
            scratch_shapes=[pltpu.VMEM((16 * chips, LANES), F32)],
            compiler_params=pltpu.CompilerParams(vmem_limit_bytes=8 * 2**20),
        )(parts)
    with jax.named_scope("exchange_documents"):
        every = lax.all_to_all(send, "dp", 0, 0, tiled=True)
    with jax.named_scope("score"):
        terms = pl.pallas_call(
            score_kernel,
            out_shape=jax.ShapeDtypeStruct((chips, 1, count), F32),
            in_specs=[VMEM] * 3,
            out_specs=VMEM,
            compiler_params=pltpu.CompilerParams(vmem_limit_bytes=8 * 2**20),
        )(query_docs[None], mine, every)
    with jax.named_scope("sum_scores"):
        terms = lax.all_to_all(terms, "ctx", 0, 0, axis_index_groups=same_core, tiled=True)
    scores = jnp.sum(terms, axis=0) / (3.0 * RANK * RANK)
    return (unit.reshape(1, -1), scores)


def solution(mesh):
    in_specs = (
        P("dp", "ctx", None),
        P("dp", "ctx", None),
        P("dp", "ctx", None),
        P("dp", "ctx", None),
        P("dp", "ctx", None),
        P("dp", None, "ctx"),
        P(),
        P(),
        P(),
        P(),
        P(),
    )
    out_specs = (P("dp", None), P("dp", None))
    return jax.shard_map(local, mesh=mesh, in_specs=in_specs, out_specs=out_specs, check_vma=False)
```

time: 110 us -> 105 us (0.955)
  waiting for transfers between devices: 7.91 us -> 5.79 us
  Pallas kernels: 14.1 us -> 12.5 us
    ppermute x1, waiting for transfers between devices: 2.02 us -> 0.01 us  [local(): lax.ppermute(keys_call(got), 'ctx', [(i, i ^ 1) for i in range(2 * chips)])]
    pallas_call x3 -> x5, Pallas kernels: 13.3 us -> 12.3 us  [the longest x1 4.17 us: message_call(): pl.pallas_call(message_kernel, out_shape=(jax.ShapeDtypeStruct((chips, to...]
  transfers between devices with their start and end apart: 2 -> 2, of which waited for: 2 -> 1; matrix products, arithmetic and copies ran while one was open for 1% -> 1% of each run, Pallas kernels for 0% -> 3%
where the time goes in v3:
time: 105 us; the launch traced here: 103 us
  blocking collectives  71.8 us (68%)
  Pallas kernels  12.5 us (12%)
  starting transfers between devices  10.8 us (10%)
  waiting for transfers between devices  5.79 us (6%)
    all_to_all x1, blocking collectives, local(): every = lax.all_to_all(send, 'dp', 0, 0, tiled=True)  29.9 us
    all_to_all x1, blocking collectives, local(): lax.all_to_all(msg, 'ctx', 0, 0, axis_index_groups=same_core, tiled=True)  29.3 us
    all_to_all x1, blocking collectives, local(): parts = lax.all_to_all(partial, 'ctx', 0, 0, tiled=True)  12.6 us
    ppermute x1, starting transfers between devices, local(): lax.ppermute(keys_call(got), 'ctx', [(i, i ^ 1) for i in range(2 * chips)])  6.8 us
    all_to_all x1, waiting for transfers between devices, local(): lax.all_to_all(terms, 'ctx', 0, 0, axis_index_groups=same_core, tiled=True)  5.78 us
    pallas_call x1, Pallas kernels, message_call(): pl.pallas_call(message_kernel, out_shape=(jax.ShapeDtypeStruct((chips, to...  4.17 us
    pallas_call x1, Pallas kernels, other_call(): pl.pallas_call(other_kernel, out_shape=jax.ShapeDtypeStruct((2 * chips, 3...  4.14 us
    all_to_all x1, starting transfers between devices, local(): lax.all_to_all(terms, 'ctx', 0, 0, axis_index_groups=same_core, tiled=True)  4 us
  transfers between devices with their start and end apart: 2, of which 1 were waited for; matrix products, arithmetic and copies ran while one was open for 1% of the time, Pallas kernels for 3%

profile of v3, /device:TPU:1, one launch (start us, length us, event | category | flops | bytes accessed | tf_op | source)
XLA Modules:
  0.0 102.8 jit_solution(1509331188149898873)
XLA Ops:
  0.6 4.2 %message.1 = (bf16[8,128,896]{2,1,0:T(8,128)(2,1)}, bf16[64,512]{1,0:T(8,128)(2,1)}) custom-call(bf16[128,2560]{1,0:T(8,128)(2,1)} %bitcast.14, bf16[128,2048]{1,0:T(8,128)(2,1)} %bitcast.15, bf16[128,1024]{1,0:T(8,128)(2,1)} %bitcast.19, bf16[128,2048]{1,0:T(8,128)(2,1)} %bitcast.16, bf16[128,2048]{1,0:T(8,128)(2,1)} %bitcast.17, f32[16,128]{1,0:T(8,128)} %bitcast.23, ...), custom_call_target="tpu_custom_call" | custom-call | tf_op jit(solution)/shard_map/message/pallas_call | solution.py:131
  4.8 29.3 %all_to_all.20.r_ref = bf16[8,128,896]{2,1,0:T(8,128)(2,1)S(1)} all-to-all(bf16[8,128,896]{2,1,0:T(8,128)(2,1)} %get-tuple-element.11), channel_id=1, replica_groups={{0,2,4,6,8,10,12,14},{1,3,5,7,9,11,13,15},{16,18,20,22,24,26,28,30},{17..., dimensions={0} | all-to-all | bytes 3670016 | tf_op jit(solution)/shard_map/exchange_heads/all_to_all | solution.py:384
  34.1 0.1 swap_cores.1
  34.1 0.0 copy-start
  34.1 6.8 %collective-permute-start = (bf16[8,128,384]{2,1,0:T(8,128)(2,1)S(1)}, bf16[8,128,384]{2,1,0:T(8,128)(2,1)S(1)}, u32[]{:S(2)}, u32[]{:S(2)}) collective-permute-start(bf16[8,128,384]{2,1,0:T(8,128)(2,1)S(1)} %swap_cores.1), channel_id=1, source_target_pairs={{0,1},{1,0},{2,3},{3,2},{4,5},{5,4},{6,7},{7,6},{8,9},{9,8},{10,11... | collective-permute-start | bytes 2359304 | tf_op jit(solution)/shard_map/swap_cores/ppermute | solution.py:386
  41.0 3.0 %own_keys.1 = (bf16[4,512,256]{2,1,0:T(8,128)(2,1)S(1)}, bf16[4,512,256]{2,1,0:T(8,128)(2,1)S(1)}, f32[2048,256]{1,0:T(8,128)S(1)}, f32[2048,128]{1,0:T(8,128)S(1)}) custom-call(bf16[8,128,896]{2,1,0:T(8,128)(2,1)S(1)} %all_to_all.20.r_ref), custom_call_target="tpu_custom_call" | custom-call | flops 4294967296 | bytes 8388608 | tf_op jit(solution)/shard_map/own_keys/pallas_call | solution.py:291
  43.9 0.0 collective-permute-done.o_ref
  44.0 0.0 copy-done
  44.0 0.0 copy-start.1
  44.0 4.1 %other_keys.1 = bf16[16,96,128]{2,1,0:T(8,128)(2,1)S(1)} custom-call(bf16[8,128,896]{2,1,0:T(8,128)(2,1)S(1)} %all_to_all.20.r_ref, bf16[8,128,384]{2,1,0:T(8,128)(2,1)S(1)} %collective-permute-done.o_ref, bf16[64,512]{1,0:T(8,128)(2,1)S(1)} %copy-done, bf16[4,512,256]{2,1,0:T(8,128)(2,1)S(1)} %get-tuple-element.13.qs, ...), custom_call_target="tpu_custom_call" | custom-call | tf_op jit(solution)/shard_map/other_keys/pallas_call | solution.py:313
  48.1 12.6 %all_to_all.21.parts_ref = bf16[16,96,128]{2,1,0:T(8,128)(2,1)S(1)} all-to-all(bf16[16,96,128]{2,1,0:T(8,128)(2,1)S(1)} %other_keys.1), channel_id=1, replica_groups=mesh['dp'=32,'ctx'=16] {'ctx'}, dimensions={0} | all-to-all | bytes 786432 | tf_op jit(solution)/shard_map/sum_parts/all_to_all | solution.py:392
  60.7 0.2 unit.1
  61.0 29.9 %all_to_all.22.every_ref = bf16[32,16,128]{2,1,0:T(8,128)(2,1)S(1)} all-to-all(bf16[32,16,128]{2,1,0:T(8,128)(2,1)S(1)} %get-tuple-element.19), channel_id=1, replica_groups=mesh['dp'=32,'ctx'=16] {'dp'}, dimensions={0} | all-to-all | bytes 262144 | tf_op jit(solution)/shard_map/exchange_documents/all_to_all | solution.py:407
  90.9 0.0 copy-done.1
  90.9 0.9 score.1
  91.8 4.0 %all-to-all-start.3 = ((f32[8,1,8]{2,1,0:T(1,128)}), f32[8,1,8]{2,1,0:T(1,128)S(1)}, u32[]{:S(2)}, u32[]{:S(2)}) async-start(f32[8,1,8]{2,1,0:T(1,128)} %score.1), calls=%async_computation.3 | async-start | bytes 8192 | tf_op jit(solution)/shard_map/sum_scores/all_to_all | solution.py:417
  95.8 0.7 reshape.18
  96.5 5.8 %all-to-all-done.3 = f32[8,1,8]{2,1,0:T(1,128)S(1)} async-done(((f32[8,1,8]{2,1,0:T(1,128)}), f32[8,1,8]{2,1,0:T(1,128)S(1)}, u32[]{:S(2)}, u32[]{:S(2)}) %all-to-all-start.3) | async-done | bytes 288 | tf_op jit(solution)/shard_map/sum_scores/all_to_all | solution.py:417
  102.3 0.5 multiply_bitcast_fusion
  (1 shorter events, 0.0 us)
Async XLA Ops:
  34.1 9.8 %copy-start = (bf16[64,512]{1,0:T(8,128)(2,1)S(1)}, bf16[64,512]{1,0:T(8,128)(2,1)}, u32[]{:S(2)}) copy-start(bf16[64,512]{1,0:T(8,128)(2,1)} %get-tuple-element.12.proj_ref) | copy-start | bytes 196612
  34.1 9.8 %collective-permute-start = (bf16[8,128,384]{2,1,0:T(8,128)(2,1)S(1)}, bf16[8,128,384]{2,1,0:T(8,128)(2,1)S(1)}, u32[]{:S(2)}, u32[]{:S(2)}) collective-permute-start(bf16[8,128,384]{2,1,0:T(8,128)(2,1)S(1)} %swap_cores.1), channel_id=1, source_target_pairs={{0,1},{1,0},{2,3},{3,2},{4,5},{5,4},{6,7},{7,6},{8,9},{9,8},{10,11... | collective-permute-start | bytes 2359304 | tf_op jit(solution)/shard_map/swap_cores/ppermute | solution.py:386
  44.0 46.9 %copy-start.1 = (s32[8]{0:T(128)S(1)}, s32[8]{0:T(128)}, u32[]{:S(2)}) copy-start(s32[8]{0:T(128)} %param.21) | copy-start | bytes 100
  91.8 10.5 %all-to-all-start.3 = ((f32[8,1,8]{2,1,0:T(1,128)}), f32[8,1,8]{2,1,0:T(1,128)S(1)}, u32[]{:S(2)}, u32[]{:S(2)}) async-start(f32[8,1,8]{2,1,0:T(1,128)} %score.1), calls=%async_computation.3 | async-start | bytes 8192 | tf_op jit(solution)/shard_map/sum_scores/all_to_all | solution.py:417

commit v4 on v3

--- a/solution.py
+++ b/solution.py
@@ -1,4 +1,3 @@
-import functools
 import math
 
 import jax
@@ -141,8 +140,13 @@
             for a in (hidden_in, keys_values, attn_out, out_grad, log_norms, proj_in_t)
         ]
         + [pltpu.SemaphoreType.DMA((13 + chips,))],
-        compiler_params=pltpu.CompilerParams(vmem_limit_bytes=60 * 2**20),
-    )(hidden_in, queries, keys_values, attn_out, out_grad, log_norms, proj_in_t, *proj_t)
+        compiler_params=pltpu.CompilerParams(vmem_limit_bytes=16 * 2**20),
+    )(
+        *[
+            pltpu.with_memory_space_constraint(a, pltpu.HBM)
+            for a in (hidden_in, queries, keys_values, attn_out, out_grad, log_norms, proj_in_t, *proj_t)
+        ]
+    )
 
 
 def part(ref, at):
@@ -333,11 +337,13 @@
     unit_ref[:, :LANES] = unit[:RANK]
     unit_ref[: RANK // 2, LANES:] = unit[RANK:, :RANK]
     unit_ref[RANK // 2 :, LANES:] = unit[RANK:, RANK:]
-    flat[: unit.shape[0], :] = unit
-    flat[unit.shape[0] :, :] = jnp.zeros((flat.shape[0] - unit.shape[0], LANES), F32)
-    depth = mine_ref.shape[0]
+    chips, depth, _ = flat.shape
+    for p in range(chips):
+        flat[p] = unit[p * depth : (p + 1) * depth]
     chip, _ = place()
-    mine = flat[pl.ds(pl.multiple_of(chip * depth, depth), depth), :]
+    mine = flat[chip]
+    rows = mine_ref.shape[0]
+    mine = jnp.concatenate([mine[r : r + rows] for r in range(0, depth, rows)], axis=1)
     mine_ref[...] = mine
     send = mine.astype(BF16)
     for i in range(send_ref.shape[0]):
@@ -356,6 +362,7 @@
     docs = every_ref.shape[0]
     terms = [jnp.sum(mine * every_ref[e].astype(F32), axis=0, keepdims=True) for e in range(docs)]
     terms = jnp.concatenate(terms, axis=0)
+    terms = sum(terms[:, i : i + LANES] for i in range(0, terms.shape[1], LANES))
     ones = jnp.ones((8, LANES), BF16)
     sums = sum(nt(ones, t) for t in split3(terms))
     asked = docs_ref[...]
@@ -395,12 +402,12 @@
             unit_kernel,
             out_shape=(
                 jax.ShapeDtypeStruct((RANK, 3 * RANK), F32),
-                jax.ShapeDtypeStruct((16, LANES), F32),
-                jax.ShapeDtypeStruct((docs, 16, LANES), BF16),
+                jax.ShapeDtypeStruct((4, 3 * LANES), F32),
+                jax.ShapeDtypeStruct((docs, 4, 3 * LANES), BF16),
             ),
             in_specs=[VMEM],
             out_specs=(VMEM, VMEM, VMEM),
-            scratch_shapes=[pltpu.VMEM((16 * chips, LANES), F32)],
+            scratch_shapes=[pltpu.VMEM((chips, 12, LANES), F32)],
             compiler_params=pltpu.CompilerParams(vmem_limit_bytes=8 * 2**20),
         )(parts)
     with jax.named_scope("exchange_documents"):

time: 105 us -> 102 us (0.971)
  Pallas kernels: 12.5 us -> 11.3 us
  starting transfers between devices: 10.8 us -> 9.72 us
    pallas_call x1, Pallas kernels: 4.17 us -> 2.91 us  [message_call(): pl.pallas_call(message_kernel, out_shape=(jax.ShapeDtypeStruct((chips, to...]
where the time goes in v4:
time: 102 us; the launch traced here: 100 us
  blocking collectives  71.4 us (70%)
  Pallas kernels  11.3 us (11%)
  starting transfers between devices  9.72 us (10%)
  waiting for transfers between devices  5.79 us (6%)
    all_to_all x1, blocking collectives, local(): lax.all_to_all(msg, 'ctx', 0, 0, axis_index_groups=same_core, tiled=True)  29.9 us
    all_to_all x1, blocking collectives, local(): every = lax.all_to_all(send, 'dp', 0, 0, tiled=True)  28.9 us
    all_to_all x1, blocking collectives, local(): parts = lax.all_to_all(partial, 'ctx', 0, 0, tiled=True)  12.6 us
    ppermute x1, starting transfers between devices, local(): lax.ppermute(keys_call(got), 'ctx', [(i, i ^ 1) for i in range(2 * chips)])  5.79 us
    all_to_all x1, waiting for transfers between devices, local(): lax.all_to_all(terms, 'ctx', 0, 0, axis_index_groups=same_core, tiled=True)  5.78 us
    pallas_call x1, Pallas kernels, other_call(): pl.pallas_call(other_kernel, out_shape=jax.ShapeDtypeStruct((2 * chips, 3...  4.14 us
    all_to_all x1, starting transfers between devices, local(): lax.all_to_all(terms, 'ctx', 0, 0, axis_index_groups=same_core, tiled=True)  3.93 us
    pallas_call x1, Pallas kernels, own_call(): pl.pallas_call(own_kernel, out_shape=(jax.ShapeDtypeStruct((groups, 2 * h...  2.99 us
  transfers between devices with their start and end apart: 2, of which 1 were waited for; matrix products, arithmetic and copies ran while one was open for 1% of the time, Pallas kernels for 3%

profile of v4, /device:TPU:1, one launch (start us, length us, event | category | flops | bytes accessed | tf_op | source)
XLA Modules:
  0.0 100.2 jit_solution(1923717417553974926)
XLA Ops:
  0.6 2.9 %message.1 = (bf16[8,128,896]{2,1,0:T(8,128)(2,1)S(1)}, bf16[64,512]{1,0:T(8,128)(2,1)S(1)}) custom-call(bf16[128,2560]{1,0:T(8,128)(2,1)} %bitcast.14, bf16[128,2048]{1,0:T(8,128)(2,1)} %bitcast.15, bf16[128,1024]{1,0:T(8,128)(2,1)} %bitcast.19, bf16[128,2048]{1,0:T(8,128)(2,1)} %bitcast.16, bf16[128,2048]{1,0:T(8,128)(2,1)} %bitcast.17, ...), custom_call_target="tpu_custom_call" | custom-call | tf_op jit(solution)/shard_map/message/pallas_call | solution.py:130
  3.5 29.9 %all_to_all.20.r_ref = bf16[8,128,896]{2,1,0:T(8,128)(2,1)S(1)} all-to-all(bf16[8,128,896]{2,1,0:T(8,128)(2,1)S(1)} %get-tuple-element.11), channel_id=1, replica_groups={{0,2,4,6,8,10,12,14},{1,3,5,7,9,11,13,15},{16,18,20,22,24,26,28,30},{17..., dimensions={0} | all-to-all | bytes 3670016 | tf_op jit(solution)/shard_map/exchange_heads/all_to_all | solution.py:391
  33.5 0.1 swap_cores.1
  33.5 5.8 %collective-permute-start = (bf16[8,128,384]{2,1,0:T(8,128)(2,1)S(1)}, bf16[8,128,384]{2,1,0:T(8,128)(2,1)S(1)}, u32[]{:S(2)}, u32[]{:S(2)}) collective-permute-start(bf16[8,128,384]{2,1,0:T(8,128)(2,1)S(1)} %swap_cores.1), channel_id=1, source_target_pairs={{0,1},{1,0},{2,3},{3,2},{4,5},{5,4},{6,7},{7,6},{8,9},{9,8},{10,11... | collective-permute-start | bytes 2359304 | tf_op jit(solution)/shard_map/swap_cores/ppermute | solution.py:393
  39.3 3.0 %own_keys.1 = (bf16[4,512,256]{2,1,0:T(8,128)(2,1)S(1)}, bf16[4,512,256]{2,1,0:T(8,128)(2,1)S(1)}, f32[2048,256]{1,0:T(8,128)S(1)}, f32[2048,128]{1,0:T(8,128)S(1)}) custom-call(bf16[8,128,896]{2,1,0:T(8,128)(2,1)S(1)} %all_to_all.20.r_ref), custom_call_target="tpu_custom_call" | custom-call | flops 4294967296 | bytes 8388608 | tf_op jit(solution)/shard_map/own_keys/pallas_call | solution.py:295
  42.3 0.0 collective-permute-done.o_ref
  42.3 0.0 copy-start
  42.4 4.1 %other_keys.1 = bf16[16,96,128]{2,1,0:T(8,128)(2,1)S(1)} custom-call(bf16[8,128,896]{2,1,0:T(8,128)(2,1)S(1)} %all_to_all.20.r_ref, bf16[8,128,384]{2,1,0:T(8,128)(2,1)S(1)} %collective-permute-done.o_ref, bf16[64,512]{1,0:T(8,128)(2,1)S(1)} %get-tuple-element.12.proj_ref, bf16[4,512,256]{2,1,0:T(8,128)(2,1)S(1)} %get-tuple-element.13.qs, ...), custom_call_target="tpu_custom_call" | custom-call | tf_op jit(solution)/shard_map/other_keys/pallas_call | solution.py:317
  46.5 12.6 %all_to_all.21.parts_ref = bf16[16,96,128]{2,1,0:T(8,128)(2,1)S(1)} all-to-all(bf16[16,96,128]{2,1,0:T(8,128)(2,1)S(1)} %other_keys.1), channel_id=1, replica_groups=mesh['dp'=32,'ctx'=16] {'ctx'}, dimensions={0} | all-to-all | bytes 786432 | tf_op jit(solution)/shard_map/sum_parts/all_to_all | solution.py:399
  59.1 0.2 unit.1
  59.3 28.9 %all_to_all.22.every_ref = bf16[32,4,384]{2,1,0:T(4,128)(2,1)S(1)} all-to-all(bf16[32,4,384]{2,1,0:T(4,128)(2,1)S(1)} %get-tuple-element.19), channel_id=1, replica_groups=mesh['dp'=32,'ctx'=16] {'dp'}, dimensions={0} | all-to-all | bytes 196608 | tf_op jit(solution)/shard_map/exchange_documents/all_to_all | solution.py:414
  88.2 0.0 copy-done
  88.2 1.0 score.1
  89.2 3.9 %all-to-all-start.3 = ((f32[8,1,8]{2,1,0:T(1,128)}), f32[8,1,8]{2,1,0:T(1,128)S(1)}, u32[]{:S(2)}, u32[]{:S(2)}) async-start(f32[8,1,8]{2,1,0:T(1,128)} %score.1), calls=%async_computation.3 | async-start | bytes 8192 | tf_op jit(solution)/shard_map/sum_scores/all_to_all | solution.py:424
  93.1 0.7 reshape.18
  93.9 5.8 %all-to-all-done.3 = f32[8,1,8]{2,1,0:T(1,128)S(1)} async-done(((f32[8,1,8]{2,1,0:T(1,128)}), f32[8,1,8]{2,1,0:T(1,128)S(1)}, u32[]{:S(2)}, u32[]{:S(2)}) %all-to-all-start.3) | async-done | bytes 288 | tf_op jit(solution)/shard_map/sum_scores/all_to_all | solution.py:424
  99.7 0.5 multiply_bitcast_fusion
  (1 shorter events, 0.0 us)
Async XLA Ops:
  33.5 8.8 %collective-permute-start = (bf16[8,128,384]{2,1,0:T(8,128)(2,1)S(1)}, bf16[8,128,384]{2,1,0:T(8,128)(2,1)S(1)}, u32[]{:S(2)}, u32[]{:S(2)}) collective-permute-start(bf16[8,128,384]{2,1,0:T(8,128)(2,1)S(1)} %swap_cores.1), channel_id=1, source_target_pairs={{0,1},{1,0},{2,3},{3,2},{4,5},{5,4},{6,7},{7,6},{8,9},{9,8},{10,11... | collective-permute-start | bytes 2359304 | tf_op jit(solution)/shard_map/swap_cores/ppermute | solution.py:393
  42.3 45.9 %copy-start = (s32[8]{0:T(128)S(1)}, s32[8]{0:T(128)}, u32[]{:S(2)}) copy-start(s32[8]{0:T(128)} %param.21) | copy-start | bytes 100
  89.2 10.4 %all-to-all-start.3 = ((f32[8,1,8]{2,1,0:T(1,128)}), f32[8,1,8]{2,1,0:T(1,128)S(1)}, u32[]{:S(2)}, u32[]{:S(2)}) async-start(f32[8,1,8]{2,1,0:T(1,128)} %score.1), calls=%async_computation.3 | async-start | bytes 8192 | tf_op jit(solution)/shard_map/sum_scores/all_to_all | solution.py:424

commit v5 on v4

--- a/solution.py
+++ b/solution.py
@@ -19,7 +19,7 @@
 
 HBM = pl.BlockSpec(memory_space=pltpu.HBM)
 
-Q_AT, D_AT, V_AT, K_AT, X_AT, WIDE = 0, 256, 512, 640, 768, 896
+Q_AT, D_AT, V_AT, K_AT, X_AT, T_AT, TALL = 0, 256, 512, 640, 768, 832, 848
 
 
 def nt(a, b):
@@ -84,42 +84,43 @@
     deltas = len(todo)
     todo += [(pin_hbm, pin_ref)] + row_parts(h_hbm, h_ref, parts) + row_parts(kv_hbm, kv_ref, parts)
     inputs = len(todo)
-    todo += [(q_hbm.at[:, pl.ds(p * two, two)], msg_ref.at[p, :, pl.ds(Q_AT, two)]) for p in range(chips)]
+    for h in range(heads):
+        cols = pl.ds(h * HEAD_DIM, HEAD_DIM)
+        todo += [(q_hbm.at[:, cols], msg_ref.at[h // 2, pl.ds(Q_AT + (h % 2) * tok, tok), :])]
     copies = start_all(todo, sems)
-    src = row_of((LANES, chips * LANES))
-    dst = lane_of((LANES, chips * LANES))
-    head = src % heads
-    to = (head // 2) * LANES + RANK + (src // heads) * 6 + (head % 2) * 3
-    to = jnp.where(src < 2 * heads, to, -8)
-    picks = [jnp.where(dst == to + j, 1.0, 0.0).astype(BF16) for j in range(3)]
     for copy in copies[:deltas]:
         copy.wait()
-    lse = jnp.concatenate([lse_ref[...], jnp.zeros((LANES - heads, tok), F32)], axis=0)
-    terms = lse.T * (-1.0 / SCALE)
+    delta = jnp.zeros((tok, LANES), F32)
     lane = lane_of((tok, LANES))
     for h in range(heads):
         cols = slice(h * HEAD_DIM, (h + 1) * HEAD_DIM)
         prod = d_ref[:, cols].astype(F32) * o_ref[:, cols].astype(F32)
-        delta = jnp.sum(prod, axis=1, keepdims=True)
-        terms = jnp.where(lane == heads + h, -delta, terms)
-    high = terms.astype(BF16)
-    rest = terms - high.astype(F32)
-    mid = rest.astype(BF16)
-    low = (rest - mid.astype(F32)).astype(BF16)
-    spread = nn(high, picks[0]) + nn(mid, picks[1]) + nn(low, picks[2])
+        delta = jnp.where(lane == h, jnp.sum(prod, axis=1, keepdims=True), delta)
+    delta = -delta.T
+    lse = lse_ref[...] * (-1.0 / SCALE)
+    terms = [half[2 * p : 2 * p + 2] for p in range(chips) for half in (lse, delta)]
+    terms = jnp.concatenate(terms, axis=0)
+    high = terms.astype(BF16).astype(F32)
+    mid = (terms - high).astype(BF16).astype(F32)
+    low = terms - high - mid
+    none = jnp.zeros((4, tok), F32)
     for p in range(chips):
-        msg_ref[p, :, D_AT:V_AT] = d_ref[:, p * two : (p + 1) * two]
+        rows = slice(4 * p, 4 * p + 4)
+        block = jnp.concatenate([high[rows], mid[rows], low[rows], none], axis=0)
+        msg_ref[p, T_AT:, :] = block.astype(BF16)
+        for h in range(2):
+            cols = slice((2 * p + h) * HEAD_DIM, (2 * p + h + 1) * HEAD_DIM)
+            msg_ref[p, D_AT + h * tok : D_AT + (h + 1) * tok, :] = d_ref[:, cols]
     for copy in copies[deltas:inputs]:
         copy.wait()
     x = nt(h_ref[...], pin_ref[...])
-    x = jnp.concatenate([x, jnp.zeros((tok, LANES - RANK), F32)], axis=1)
+    x = jnp.concatenate([x[: tok // 2], x[tok // 2 :]], axis=1).astype(BF16)
     kv_cols = KV_HEADS * HEAD_DIM
     for p in range(chips):
         kv = 2 * p // group
-        msg_ref[p, :, V_AT:K_AT] = kv_ref[:, kv_cols + kv * HEAD_DIM : kv_cols + (kv + 1) * HEAD_DIM]
-        msg_ref[p, :, K_AT:X_AT] = kv_ref[:, kv * HEAD_DIM : (kv + 1) * HEAD_DIM]
-        block = x + spread[:, p * LANES : (p + 1) * LANES]
-        msg_ref[p, :, X_AT:] = block.astype(BF16)
+        msg_ref[p, V_AT:K_AT, :] = kv_ref[:, kv_cols + kv * HEAD_DIM : kv_cols + (kv + 1) * HEAD_DIM]
+        msg_ref[p, K_AT:X_AT, :] = kv_ref[:, kv * HEAD_DIM : (kv + 1) * HEAD_DIM]
+        msg_ref[p, X_AT:T_AT, :] = x
     for copy in copies[inputs:]:
         copy.wait()
 
@@ -130,7 +131,7 @@
     return pl.pallas_call(
         message_kernel,
         out_shape=(
-            jax.ShapeDtypeStruct((chips, tok, WIDE), BF16),
+            jax.ShapeDtypeStruct((chips, TALL, LANES), BF16),
             jax.ShapeDtypeStruct((RANK, 4 * HEAD_DIM), BF16),
         ),
         in_specs=[HBM] * 10,
@@ -139,7 +140,7 @@
             pltpu.VMEM(a.shape, a.dtype)
             for a in (hidden_in, keys_values, attn_out, out_grad, log_norms, proj_in_t)
         ]
-        + [pltpu.SemaphoreType.DMA((13 + chips,))],
+        + [pltpu.SemaphoreType.DMA((13 + 2 * chips,))],
         compiler_params=pltpu.CompilerParams(vmem_limit_bytes=16 * 2**20),
     )(
         *[
@@ -150,21 +151,27 @@
 
 
 def part(ref, at):
-    return ref[:, :, at : at + LANES].reshape(ref.shape[0] * ref.shape[1], LANES)
+    return ref[:, at : at + LANES, :].reshape(ref.shape[0] * LANES, LANES)
 
 
 def head_at(index):
     return pl.ds(pl.multiple_of(index * HEAD_DIM, HEAD_DIM), HEAD_DIM)
 
 
-def load_keys(ref, base, kt, vt):
-    rows = ref.shape[0] * ref.shape[1]
+def load_keys(ref, base, kt, vt, kx):
+    rows = ref.shape[0] * LANES
     for to, at in ((kt, K_AT), (vt, V_AT)):
         to[:LANES, :] = part(ref, at - base).T
         to[LANES:, :] = jnp.ones((LANES, rows), BF16)
-
-
-def group_terms(g, tok, base, seen_of, qs, ds, keys_ref, kt, vt, ps, dss):
+    kx[:, :LANES] = part(ref, K_AT - base)
+    half = LANES // 2
+    for b in range(ref.shape[0]):
+        x = ref[b, X_AT - base : T_AT - base, :]
+        kx[b * LANES : b * LANES + half, LANES:] = x
+        kx[b * LANES + half : (b + 1) * LANES, LANES:] = pltpu.roll(x.astype(F32), half, 1).astype(BF16)
+
+
+def group_terms(g, tok, seen_of, qs, ds, kx, kt, vt, ps, dss):
     half = 2 * tok
     upto = (g + 1) * half
     fold = SCALE * math.log2(math.e)
@@ -179,46 +186,47 @@
             dscores = probs * nn(ds[g, rr], vt[:, cols])
             ps[rr, cols] = probs.astype(BF16)
             dss[rr, cols] = dscores.astype(BF16)
-    keys = keys_ref[: 2 * (g + 1), :, K_AT - base :].reshape(upto, 2 * LANES)
-    return nn(ps[:, :upto], keys[:, LANES:]), nn(dss[:, :upto], keys)
-
-
-def own_kernel(r_ref, qs, ds, acc, acc_v, kt, vt, ps, dss):
-    blocks, tok, _ = r_ref.shape
+    return nn(ps[:, :upto], kx[:upto, LANES:]), nn(dss[:, :upto], kx[:upto, :])
+
+
+def own_kernel(r_ref, qs, ds, acc, acc_v, xs, kt, vt, kx, ps, dss):
+    blocks = r_ref.shape[0]
+    tok = LANES
     rows = blocks * tok
     half = 2 * tok
     groups = rows // half
-    lane = lane_of((rows, LANES))
-    xl = part(r_ref, X_AT)
-    none = jnp.zeros_like(xl)
-    load_keys(r_ref, 0, kt, vt)
-    for h in range(2):
-        for ref, at, kind in ((qs, Q_AT, 0), (ds, D_AT, 1)):
-            val = part(r_ref, at + h * LANES)
-            start = RANK + kind * 6 + h * 3
-            side = jnp.where((lane >= start) & (lane < start + 3), xl, none)
-            for g in range(groups):
-                ref[g, h * half : (h + 1) * half, :LANES] = val[g * half : (g + 1) * half]
-                ref[g, h * half : (h + 1) * half, LANES:] = side[g * half : (g + 1) * half]
+    load_keys(r_ref, 0, kt, vt, kx)
+    xs[...] = kx[:, LANES:]
+    lane = lane_of((tok, LANES))
+    for b in range(blocks):
+        terms = r_ref[b, T_AT:, :].astype(F32)
+        terms = jnp.concatenate([terms, jnp.zeros((LANES - terms.shape[0], tok), F32)], axis=0).T
+        g, at = b // 2, b % 2 * tok
+        for h in range(2):
+            to = slice(h * half + at, h * half + at + tok)
+            for ref, start, kind in ((qs, Q_AT, 0), (ds, D_AT, 1)):
+                mine = (lane % 4 == 2 * kind + h) & (lane < 12)
+                ref[g, to, :LANES] = r_ref[b, start + h * tok : start + (h + 1) * tok, :]
+                ref[g, to, LANES:] = jnp.where(mine, terms, 0.0).astype(BF16)
     for g in range(groups):
         to = slice(2 * g * half, 2 * (g + 1) * half)
-        acc_v[to], acc[to] = group_terms(g, tok, 0, lambda r, c: c <= r, qs, ds, r_ref, kt, vt, ps, dss)
-
-
-def other_kernel(r_ref, o_ref, proj_ref, qs, ds, acc, acc_v, out_ref, kt, vt, ps, dss, rq, rk, rv):
+        acc_v[to], acc[to] = group_terms(g, tok, lambda r, c: c <= r, qs, ds, kx, kt, vt, ps, dss)
+
+
+def other_kernel(r_ref, o_ref, proj_ref, qs, ds, acc, acc_v, xs, out_ref, kt, vt, kx, ps, dss, rq, rk, rv):
     _, core = place()
-    blocks, tok, _ = r_ref.shape
-    rows = blocks * tok
+    tok = LANES
+    rows = r_ref.shape[0] * tok
     half = 2 * tok
     groups = rows // half
-    load_keys(o_ref, V_AT, kt, vt)
+    load_keys(o_ref, V_AT, kt, vt, kx)
 
     def seen_of(r, c):
         return (c // tok) < (r // tok) + core
 
     for g in range(groups):
         to = slice(2 * g * half, 2 * (g + 1) * half)
-        for_v, for_qk = group_terms(g, tok, V_AT, seen_of, qs, ds, o_ref, kt, vt, ps, dss)
+        for_v, for_qk = group_terms(g, tok, seen_of, qs, ds, kx, kt, vt, ps, dss)
         for_v, for_qk = for_v + acc_v[to], for_qk + acc[to]
         for ref, val in ((rv, for_v), (rk, for_qk[:, LANES:]), (rq, for_qk[:, :LANES])):
             high, low = split2(val)
@@ -235,7 +243,7 @@
         high, low = split2(a)
         return product(high, b) + product(low, b)
 
-    xl = part(r_ref, X_AT)
+    xl = xs[...]
     zero = jnp.zeros((RANK, LANES), F32)
     out_q = zero
     mk = jnp.zeros((LANES, LANES), F32)
@@ -264,14 +272,13 @@
 
 
 def keys_kernel(r_ref, out_ref):
-    out_ref[...] = r_ref[:, :, V_AT:]
+    out_ref[...] = r_ref[:, V_AT:T_AT, :]
 
 
 def keys_call(got):
-    chips, tok, _ = got.shape
     return pl.pallas_call(
         keys_kernel,
-        out_shape=jax.ShapeDtypeStruct((chips, tok, WIDE - V_AT), BF16),
+        out_shape=jax.ShapeDtypeStruct((got.shape[0], T_AT - V_AT, LANES), BF16),
         in_specs=[VMEM],
         out_specs=VMEM,
         compiler_params=pltpu.CompilerParams(vmem_limit_bytes=8 * 2**20),
@@ -282,15 +289,16 @@
     return [
         pltpu.VMEM((2 * LANES, rows), BF16),
         pltpu.VMEM((2 * LANES, rows), BF16),
+        pltpu.VMEM((rows, 2 * LANES), BF16),
         pltpu.VMEM((2 * half, rows), BF16),
         pltpu.VMEM((2 * half, rows), BF16),
     ]
 
 
 def own_call(got):
-    chips, tok, _ = got.shape
-    rows = chips * tok
-    half = 2 * tok
+    chips = got.shape[0]
+    rows = chips * LANES
+    half = 2 * LANES
     groups = rows // half
     return pl.pallas_call(
         own_kernel,
@@ -299,9 +307,10 @@
             jax.ShapeDtypeStruct((groups, 2 * half, 2 * LANES), BF16),
             jax.ShapeDtypeStruct((2 * rows, 2 * LANES), F32),
             jax.ShapeDtypeStruct((2 * rows, LANES), F32),
+            jax.ShapeDtypeStruct((rows, LANES), BF16),
         ),
         in_specs=[VMEM],
-        out_specs=(VMEM,) * 4,
+        out_specs=(VMEM,) * 5,
         scratch_shapes=attention_scratch(rows, half),
         compiler_params=pltpu.CompilerParams(vmem_limit_bytes=24 * 2**20),
         cost_estimate=pl.CostEstimate(
@@ -311,13 +320,13 @@
 
 
 def other_call(got, other, proj, saved):
-    chips, tok, _ = got.shape
-    rows = chips * tok
-    half = 2 * tok
+    chips = got.shape[0]
+    rows = chips * LANES
+    half = 2 * LANES
     return pl.pallas_call(
         other_kernel,
         out_shape=jax.ShapeDtypeStruct((2 * chips, 3 * RANK // 2, LANES), BF16),
-        in_specs=[VMEM] * 7,
+        in_specs=[VMEM] * 8,
         out_specs=VMEM,
         scratch_shapes=attention_scratch(rows, half) + [pltpu.VMEM((2 * rows, 2 * LANES), BF16)] * 3,
         compiler_params=pltpu.CompilerParams(vmem_limit_bytes=24 * 2**20),

time: 102 us -> 100 us (0.980)
  no operation moved by 1% of the time
where the time goes in v5:
time: 100 us; the launch traced here: 98.9 us
  blocking collectives  70.9 us (71%)
  Pallas kernels  11 us (11%)
  starting transfers between devices  9.18 us (9%)
  waiting for transfers between devices  5.79 us (6%)
    all_to_all x1, blocking collectives, local(): lax.all_to_all(msg, 'ctx', 0, 0, axis_index_groups=same_core, tiled=True)  29.4 us
    all_to_all x1, blocking collectives, local(): every = lax.all_to_all(send, 'dp', 0, 0, tiled=True)  28.9 us
    all_to_all x1, blocking collectives, local(): parts = lax.all_to_all(partial, 'ctx', 0, 0, tiled=True)  12.6 us
    all_to_all x1, waiting for transfers between devices, local(): lax.all_to_all(terms, 'ctx', 0, 0, axis_index_groups=same_core, tiled=True)  5.78 us
    ppermute x1, starting transfers between devices, local(): lax.ppermute(keys_call(got), 'ctx', [(i, i ^ 1) for i in range(2 * chips)])  5.3 us
    pallas_call x1, Pallas kernels, other_call(): pl.pallas_call(other_kernel, out_shape=jax.ShapeDtypeStruct((2 * chips, 3...  4.16 us
    all_to_all x1, starting transfers between devices, local(): lax.all_to_all(terms, 'ctx', 0, 0, axis_index_groups=same_core, tiled=True)  3.89 us
    pallas_call x1, Pallas kernels, own_call(): pl.pallas_call(own_kernel, out_shape=(jax.ShapeDtypeStruct((groups, 2 * h...  3.11 us
  transfers between devices with their start and end apart: 2, of which 1 were waited for; matrix products, arithmetic and copies ran while one was open for 1% of the time, Pallas kernels for 3%

profile of v5, /device:TPU:1, one launch (start us, length us, event | category | flops | bytes accessed | tf_op | source)
XLA Modules:
  0.0 98.9 jit_solution(13400573800593969176)
XLA Ops:
  0.6 2.5 %message.1 = (bf16[8,848,128]{2,1,0:T(8,128)(2,1)S(1)}, bf16[64,512]{1,0:T(8,128)(2,1)S(1)}) custom-call(bf16[128,2560]{1,0:T(8,128)(2,1)} %bitcast.14, bf16[128,2048]{1,0:T(8,128)(2,1)} %bitcast.15, bf16[128,1024]{1,0:T(8,128)(2,1)} %bitcast.19, bf16[128,2048]{1,0:T(8,128)(2,1)} %bitcast.16, bf16[128,2048]{1,0:T(8,128)(2,1)} %bitcast.17, ...), custom_call_target="tpu_custom_call" | custom-call | tf_op jit(solution)/shard_map/message/pallas_call | solution.py:131
  3.1 29.4 %all_to_all.20.r_ref = bf16[8,848,128]{2,1,0:T(8,128)(2,1)S(1)} all-to-all(bf16[8,848,128]{2,1,0:T(8,128)(2,1)S(1)} %get-tuple-element.12), channel_id=1, replica_groups={{0,2,4,6,8,10,12,14},{1,3,5,7,9,11,13,15},{16,18,20,22,24,26,28,30},{17..., dimensions={0} | all-to-all | bytes 3473408 | tf_op jit(solution)/shard_map/exchange_heads/all_to_all | solution.py:400
  32.6 5.3 %collective-permute-start = (bf16[8,320,128]{2,1,0:T(8,128)(2,1)S(1)}, bf16[8,320,128]{2,1,0:T(8,128)(2,1)S(1)}, u32[]{:S(2)}, u32[]{:S(2)}) collective-permute-start(bf16[8,320,128]{2,1,0:T(8,128)(2,1)S(1)} %swap_cores.1), channel_id=1, source_target_pairs={{0,1},{1,0},{2,3},{3,2},{4,5},{5,4},{6,7},{7,6},{8,9},{9,8},{10,11... | collective-permute-start | bytes 1966088 | tf_op jit(solution)/shard_map/swap_cores/ppermute | solution.py:402
  37.9 3.1 %own_keys.1 = (bf16[4,512,256]{2,1,0:T(8,128)(2,1)S(1)}, bf16[4,512,256]{2,1,0:T(8,128)(2,1)S(1)}, f32[2048,256]{1,0:T(8,128)S(1)}, f32[2048,128]{1,0:T(8,128)S(1)}, bf16[1024,128]{1,0:T(8,128)(2,1)S(1)}) custom-call(bf16[8,848,128]{2,1,0:T(8,128)(2,1)S(1)} %all_to_all.20.r_ref), custom_call_target="tpu_custom_call" | custom-call | flops 4294967296 | bytes 8388608 | tf_op jit(solution)/shard_map/own_keys/pallas_call | solution.py:303
  41.0 0.0 collective-permute-done.o_ref
  41.0 0.0 copy-start
  41.0 4.2 %other_keys.1 = bf16[16,96,128]{2,1,0:T(8,128)(2,1)S(1)} custom-call(bf16[8,848,128]{2,1,0:T(8,128)(2,1)S(1)} %all_to_all.20.r_ref, bf16[8,320,128]{2,1,0:T(8,128)(2,1)S(1)} %collective-permute-done.o_ref, bf16[64,512]{1,0:T(8,128)(2,1)S(1)} %get-tuple-element.13.proj_ref, bf16[4,512,256]{2,1,0:T(8,128)(2,1)S(1)} %get-tuple-element.14.qs, ...), custom_call_target="tpu_custom_call" | custom-call | tf_op jit(solution)/shard_map/other_keys/pallas_call | solution.py:326
  45.2 12.6 %all_to_all.21.parts_ref = bf16[16,96,128]{2,1,0:T(8,128)(2,1)S(1)} all-to-all(bf16[16,96,128]{2,1,0:T(8,128)(2,1)S(1)} %other_keys.1), channel_id=1, replica_groups=mesh['dp'=32,'ctx'=16] {'ctx'}, dimensions={0} | all-to-all | bytes 786432 | tf_op jit(solution)/shard_map/sum_parts/all_to_all | solution.py:408
  57.8 0.2 unit.1
  58.0 28.9 %all_to_all.22.every_ref = bf16[32,4,384]{2,1,0:T(4,128)(2,1)S(1)} all-to-all(bf16[32,4,384]{2,1,0:T(4,128)(2,1)S(1)} %get-tuple-element.21), channel_id=1, replica_groups=mesh['dp'=32,'ctx'=16] {'dp'}, dimensions={0} | all-to-all | bytes 196608 | tf_op jit(solution)/shard_map/exchange_documents/all_to_all | solution.py:423
  86.9 0.0 copy-done
  86.9 1.0 score.1
  87.9 3.9 %all-to-all-start.3 = ((f32[8,1,8]{2,1,0:T(1,128)}), f32[8,1,8]{2,1,0:T(1,128)S(1)}, u32[]{:S(2)}, u32[]{:S(2)}) async-start(f32[8,1,8]{2,1,0:T(1,128)} %score.1), calls=%async_computation.3 | async-start | bytes 8192 | tf_op jit(solution)/shard_map/sum_scores/all_to_all | solution.py:433
  91.8 0.7 reshape.18
  92.5 5.8 %all-to-all-done.3 = f32[8,1,8]{2,1,0:T(1,128)S(1)} async-done(((f32[8,1,8]{2,1,0:T(1,128)}), f32[8,1,8]{2,1,0:T(1,128)S(1)}, u32[]{:S(2)}, u32[]{:S(2)}) %all-to-all-start.3) | async-done | bytes 288 | tf_op jit(solution)/shard_map/sum_scores/all_to_all | solution.py:433
  98.3 0.5 multiply_bitcast_fusion
  (2 shorter events, 0.1 us)
Async XLA Ops:
  32.6 8.4 %collective-permute-start = (bf16[8,320,128]{2,1,0:T(8,128)(2,1)S(1)}, bf16[8,320,128]{2,1,0:T(8,128)(2,1)S(1)}, u32[]{:S(2)}, u32[]{:S(2)}) collective-permute-start(bf16[8,320,128]{2,1,0:T(8,128)(2,1)S(1)} %swap_cores.1), channel_id=1, source_target_pairs={{0,1},{1,0},{2,3},{3,2},{4,5},{5,4},{6,7},{7,6},{8,9},{9,8},{10,11... | collective-permute-start | bytes 1966088 | tf_op jit(solution)/shard_map/swap_cores/ppermute | solution.py:402
  41.0 45.9 %copy-start = (s32[8]{0:T(128)S(1)}, s32[8]{0:T(128)}, u32[]{:S(2)}) copy-start(s32[8]{0:T(128)} %param.21) | copy-start | bytes 100
  87.9 10.4 %all-to-all-start.3 = ((f32[8,1,8]{2,1,0:T(1,128)}), f32[8,1,8]{2,1,0:T(1,128)S(1)}, u32[]{:S(2)}, u32[]{:S(2)}) async-start(f32[8,1,8]{2,1,0:T(1,128)} %score.1), calls=%async_computation.3 | async-start | bytes 8192 | tf_op jit(solution)/shard_map/sum_scores/all_to_all | solution.py:433

commit v6 on v5

--- a/solution.py
+++ b/solution.py
@@ -1,3 +1,4 @@
+import functools
 import math
 
 import jax
@@ -213,7 +214,7 @@
         acc_v[to], acc[to] = group_terms(g, tok, lambda r, c: c <= r, qs, ds, kx, kt, vt, ps, dss)
 
 
-def other_kernel(r_ref, o_ref, proj_ref, qs, ds, acc, acc_v, xs, out_ref, kt, vt, kx, ps, dss, rq, rk, rv):
+def other_kernel(r_ref, o_ref, proj_ref, qs, ds, acc, acc_v, xs, out_ref, kt, vt, kx, ps, dss, rq, rk, rv, flat):
     _, core = place()
     tok = LANES
     rows = r_ref.shape[0] * tok
@@ -265,10 +266,19 @@
     tv = jnp.concatenate([tv, zero], axis=0).T[:RANK]
     low_lanes = lane_of((RANK, LANES)) < RANK
     top = jnp.where(low_lanes, out_q * SCALE, pltpu.roll(tk, RANK, 1))
-    bottom = jnp.where(low_lanes[: RANK // 2], tv[: RANK // 2], pltpu.roll(tv, RANK, 1)[RANK // 2 :])
-    packed = jnp.concatenate([top, bottom], axis=0).astype(BF16)
+    flat[:RANK] = top
+    flat[RANK : 2 * RANK] = tv
+    rows = RANK // 2
+    low_lanes = low_lanes[:rows]
+    even, odd = flat[pl.ds(0, rows, stride=2), :], flat[pl.ds(1, rows, stride=2), :]
+    even_v, odd_v = flat[pl.ds(RANK, rows, stride=2), :], flat[pl.ds(RANK + 1, rows, stride=2), :]
+    odd = pltpu.roll(odd, RANK, 1)
+    flat[pl.ds(0, rows, stride=3), :] = even
+    flat[pl.ds(1, rows, stride=3), :] = jnp.where(low_lanes, even_v, odd)
+    flat[pl.ds(2, rows, stride=3), :] = jnp.where(low_lanes, odd, pltpu.roll(odd_v, RANK, 1))
+    depth = out_ref.shape[1]
     for i in range(out_ref.shape[0]):
-        out_ref[i] = packed
+        out_ref[i] = flat[i * depth : (i + 1) * depth]
 
 
 def keys_kernel(r_ref, out_ref):
@@ -325,38 +335,17 @@
     half = 2 * LANES
     return pl.pallas_call(
         other_kernel,
-        out_shape=jax.ShapeDtypeStruct((2 * chips, 3 * RANK // 2, LANES), BF16),
+        out_shape=jax.ShapeDtypeStruct((2 * chips, 3 * RANK // 2 // (2 * chips), LANES), F32),
         in_specs=[VMEM] * 8,
         out_specs=VMEM,
-        scratch_shapes=attention_scratch(rows, half) + [pltpu.VMEM((2 * rows, 2 * LANES), BF16)] * 3,
+        scratch_shapes=attention_scratch(rows, half) + [pltpu.VMEM((2 * rows, 2 * LANES), BF16)] * 3
+        + [pltpu.VMEM((2 * RANK, LANES), F32)],
         compiler_params=pltpu.CompilerParams(vmem_limit_bytes=24 * 2**20),
     )(got, other, proj, *saved)
 
 
 def attention_call(got, other, proj):
     return other_call(got, other, proj, own_call(got))
-
-
-def unit_kernel(parts_ref, unit_ref, mine_ref, send_ref, flat):
-    total = parts_ref[0].astype(F32)
-    for i in range(1, parts_ref.shape[0]):
-        total = total + parts_ref[i].astype(F32)
-    mean = jnp.sum(jnp.sum(total * total, axis=0, keepdims=True), axis=1, keepdims=True) / (3.0 * RANK * RANK)
-    unit = total / jnp.sqrt(mean + 1e-6)
-    unit_ref[:, :LANES] = unit[:RANK]
-    unit_ref[: RANK // 2, LANES:] = unit[RANK:, :RANK]
-    unit_ref[RANK // 2 :, LANES:] = unit[RANK:, RANK:]
-    chips, depth, _ = flat.shape
-    for p in range(chips):
-        flat[p] = unit[p * depth : (p + 1) * depth]
-    chip, _ = place()
-    mine = flat[chip]
-    rows = mine_ref.shape[0]
-    mine = jnp.concatenate([mine[r : r + rows] for r in range(0, depth, rows)], axis=1)
-    mine_ref[...] = mine
-    send = mine.astype(BF16)
-    for i in range(send_ref.shape[0]):
-        send_ref[i] = send
 
 
 def split3(a):
@@ -366,19 +355,59 @@
     return high, mid, low
 
 
-def score_kernel(docs_ref, mine_ref, every_ref, out_ref):
+def slice_kernel(parts_ref, mine_ref, send_ref):
+    mine = parts_ref[0]
+    for i in range(1, parts_ref.shape[0]):
+        mine = mine + parts_ref[i]
+    mine_ref[...] = mine
+    rows = send_ref.shape[1]
+    wide = [mine[r : r + rows] for r in range(0, mine.shape[0], rows)]
+    send = jnp.concatenate(wide, axis=1).astype(BF16)
+    for i in range(send_ref.shape[0]):
+        send_ref[i] = send
+
+
+def dot_kernel(mine_ref, every_ref, out_ref):
+    docs, rows, _ = every_ref.shape
     mine = mine_ref[...]
-    docs = every_ref.shape[0]
-    terms = [jnp.sum(mine * every_ref[e].astype(F32), axis=0, keepdims=True) for e in range(docs)]
-    terms = jnp.concatenate(terms, axis=0)
+    wide = jnp.concatenate([mine[r : r + rows] for r in range(0, mine.shape[0], rows)], axis=1)
+    terms, squares = [], []
+    for e in range(docs):
+        other = every_ref[e].astype(F32)
+        for to, product in ((terms, wide * other), (squares, other * other)):
+            to.append(jnp.sum(product, axis=0, keepdims=True))
+    terms = jnp.concatenate(terms + squares, axis=0)
     terms = sum(terms[:, i : i + LANES] for i in range(0, terms.shape[1], LANES))
+    terms = jnp.concatenate([terms, jnp.zeros((LANES - 2 * docs, LANES), F32)], axis=0)
     ones = jnp.ones((8, LANES), BF16)
     sums = sum(nt(ones, t) for t in split3(terms))
+    depth = mine.shape[0]
+    for i in range(out_ref.shape[0]):
+        out_ref[i, :depth] = mine
+        out_ref[i, depth:] = sums[: out_ref.shape[1] - depth]
+
+
+def unit_kernel(docs, all_ref, docs_ref, unit_ref, score_ref):
+    count, depth = all_ref.shape[0], unit_ref.shape[0] // all_ref.shape[0]
+    size = 3.0 * RANK * RANK
+    square = jnp.zeros((depth, LANES), F32)
+    sums = jnp.zeros((all_ref.shape[1] - depth, LANES), F32)
+    for i in range(count):
+        part = all_ref[i]
+        square = square + part[:depth] * part[:depth]
+        sums = sums + part[depth:]
+    mean = jnp.sum(jnp.sum(square, axis=0, keepdims=True), axis=1, keepdims=True) / size
+    norm = jnp.sqrt(mean + 1e-6)
+    for i in range(count):
+        unit_ref[i * depth : (i + 1) * depth] = all_ref[i, :depth] / norm
+    sums = sums[:1]
+    other = jnp.sqrt(sums[:, docs : 2 * docs] / size + 1e-6)
+    factor = 1.0 / (norm * size) * (1.0 / other)
+    scores = jnp.where(factor == 0.0, 0.0, sums[:, :docs] * factor)
     asked = docs_ref[...]
     picks = jnp.where(row_of((docs, asked.shape[1])) == asked, 1.0, 0.0).astype(BF16)
-    picked = sum(nn(t, picks) for t in split3(sums))
-    for i in range(out_ref.shape[0]):
-        out_ref[i] = picked[:1]
+    scores = jnp.concatenate([scores, jnp.zeros((7, docs), F32)], axis=0)
+    score_ref[...] = sum(nn(t, picks) for t in split3(scores))[:1]
 
 
 def local(
@@ -388,7 +417,6 @@
     heads = log_norms.shape[1]
     chips = heads // 2
     docs = lax.axis_size("dp")
-    count = query_docs.shape[0]
     same_core = [[2 * p + c for p in range(chips)] for c in range(2)]
 
     with jax.named_scope("message"):
@@ -404,34 +432,44 @@
         saved = own_call(got)
     with jax.named_scope("other_keys"):
         partial = other_call(got, other, proj, saved)
+    small = pltpu.CompilerParams(vmem_limit_bytes=8 * 2**20)
+    with jax.named_scope("exchange_parts"):
+        parts = lax.all_to_all(partial, "ctx", 0, 0, tiled=True)
     with jax.named_scope("sum_parts"):
-        parts = lax.all_to_all(partial, "ctx", 0, 0, tiled=True)
-    with jax.named_scope("unit"):
-        unit, mine, send = pl.pallas_call(
-            unit_kernel,
+        depth = partial.shape[1]
+        mine, send = pl.pallas_call(
+            slice_kernel,
             out_shape=(
-                jax.ShapeDtypeStruct((RANK, 3 * RANK), F32),
-                jax.ShapeDtypeStruct((4, 3 * LANES), F32),
-                jax.ShapeDtypeStruct((docs, 4, 3 * LANES), BF16),
+                jax.ShapeDtypeStruct((depth, LANES), F32),
+                jax.ShapeDtypeStruct((docs, 2, depth // 2 * LANES), BF16),
             ),
             in_specs=[VMEM],
-            out_specs=(VMEM, VMEM, VMEM),
-            scratch_shapes=[pltpu.VMEM((chips, 12, LANES), F32)],
-            compiler_params=pltpu.CompilerParams(vmem_limit_bytes=8 * 2**20),
+            out_specs=(VMEM, VMEM),
+            compiler_params=small,
         )(parts)
     with jax.named_scope("exchange_documents"):
         every = lax.all_to_all(send, "dp", 0, 0, tiled=True)
-    with jax.named_scope("score"):
+    with jax.named_scope("dots"):
         terms = pl.pallas_call(
-            score_kernel,
-            out_shape=jax.ShapeDtypeStruct((chips, 1, count), F32),
-            in_specs=[VMEM] * 3,
+            dot_kernel,
+            out_shape=jax.ShapeDtypeStruct((2 * chips, 8, LANES), F32),
+            in_specs=[VMEM] * 2,
             out_specs=VMEM,
-            compiler_params=pltpu.CompilerParams(vmem_limit_bytes=8 * 2**20),
-        )(query_docs[None], mine, every)
-    with jax.named_scope("sum_scores"):
-        terms = lax.all_to_all(terms, "ctx", 0, 0, axis_index_groups=same_core, tiled=True)
-    scores = jnp.sum(terms, axis=0) / (3.0 * RANK * RANK)
+            compiler_params=small,
+        )(mine, every)
+    with jax.named_scope("exchange_slices"):
+        terms = lax.all_to_all(terms, "ctx", 0, 0, tiled=True)
+    with jax.named_scope("unit"):
+        unit, scores = pl.pallas_call(
+            functools.partial(unit_kernel, docs),
+            out_shape=(
+                jax.ShapeDtypeStruct((3 * RANK // 2, LANES), F32),
+                jax.ShapeDtypeStruct((1, query_docs.shape[0]), F32),
+            ),
+            in_specs=[VMEM] * 2,
+            out_specs=(VMEM, VMEM),
+            compiler_params=small,
+        )(terms, query_docs[None])
     return (unit.reshape(1, -1), scores)
 
 

time: 100 us -> 97 us (0.970)
  blocking collectives: 70.9 us -> 79.5 us
  waiting for transfers between devices: 5.79 us -> 0.01 us
  starting transfers between devices: 9.18 us -> 5.3 us
    all_to_all x0 -> x1, blocking collectives: none -> 12.1 us  [local(): terms = lax.all_to_all(terms, 'ctx', 0, 0, tiled=True)]
    all_to_all x1 -> x0, waiting for transfers between devices: 5.78 us -> none  [local(): lax.all_to_all(terms, 'ctx', 0, 0, axis_index_groups=same_core, tiled=True)]
    all_to_all x1 -> x0, starting transfers between devices: 3.89 us -> none  [local(): lax.all_to_all(terms, 'ctx', 0, 0, axis_index_groups=same_core, tiled=True)]
    all_to_all x1, blocking collectives: 12.6 us -> 9.99 us  [local(): parts = lax.all_to_all(partial, 'ctx', 0, 0, tiled=True)]
  transfers between devices with their start and end apart: 2 -> 1, of which waited for: 1 -> 0; matrix products, arithmetic and copies ran while one was open for 1% -> 0% of each run, Pallas kernels for 3% -> 3%
where the time goes in v6:
time: 97 us; the launch traced here: 96.7 us
  blocking collectives  79.5 us (82%)
  Pallas kernels  11.2 us (12%)
  starting transfers between devices  5.3 us (5%)
    all_to_all x1, blocking collectives, local(): lax.all_to_all(msg, 'ctx', 0, 0, axis_index_groups=same_core, tiled=True)  29.4 us
    all_to_all x1, blocking collectives, local(): every = lax.all_to_all(send, 'dp', 0, 0, tiled=True)  28 us
    all_to_all x1, blocking collectives, local(): terms = lax.all_to_all(terms, 'ctx', 0, 0, tiled=True)  12.1 us
    all_to_all x1, blocking collectives, local(): parts = lax.all_to_all(partial, 'ctx', 0, 0, tiled=True)  9.99 us
    ppermute x1, starting transfers between devices, local(): lax.ppermute(keys_call(got), 'ctx', [(i, i ^ 1) for i in range(2 * chips)])  5.3 us
    pallas_call x1, Pallas kernels, other_call(): pl.pallas_call(other_kernel, out_shape=jax.ShapeDtypeStruct((2 * chips, 3...  4.16 us
    pallas_call x1, Pallas kernels, own_call(): pl.pallas_call(own_kernel, out_shape=(jax.ShapeDtypeStruct((groups, 2 * h...  3.11 us
    pallas_call x1, Pallas kernels, message_call(): pl.pallas_call(message_kernel, out_shape=(jax.ShapeDtypeStruct((chips, TA...  2.5 us
  transfers between devices with their start and end apart: 1, of which 0 were waited for; matrix products, arithmetic and copies ran while one was open for 0% of the time, Pallas kernels for 3%

profile of v6, /device:TPU:1, one launch (start us, length us, event | category | flops | bytes accessed | tf_op | source)
XLA Modules:
  0.0 96.7 jit_solution(8649939557368645309)
XLA Ops:
  0.6 2.5 %message.1 = (bf16[8,848,128]{2,1,0:T(8,128)(2,1)S(1)}, bf16[64,512]{1,0:T(8,128)(2,1)S(1)}) custom-call(bf16[128,2560]{1,0:T(8,128)(2,1)} %bitcast.13, bf16[128,2048]{1,0:T(8,128)(2,1)} %bitcast.14, bf16[128,1024]{1,0:T(8,128)(2,1)} %bitcast.18, bf16[128,2048]{1,0:T(8,128)(2,1)} %bitcast.15, bf16[128,2048]{1,0:T(8,128)(2,1)} %bitcast.16, ...), custom_call_target="tpu_custom_call" | custom-call | tf_op jit(solution)/shard_map/message/pallas_call | solution.py:132
  3.1 29.4 %all_to_all.20.r_ref = bf16[8,848,128]{2,1,0:T(8,128)(2,1)S(1)} all-to-all(bf16[8,848,128]{2,1,0:T(8,128)(2,1)S(1)} %get-tuple-element.13), channel_id=1, replica_groups={{0,2,4,6,8,10,12,14},{1,3,5,7,9,11,13,15},{16,18,20,22,24,26,28,30},{17..., dimensions={0} | all-to-all | bytes 3473408 | tf_op jit(solution)/shard_map/exchange_heads/all_to_all | solution.py:428
  32.6 5.3 %collective-permute-start = (bf16[8,320,128]{2,1,0:T(8,128)(2,1)S(1)}, bf16[8,320,128]{2,1,0:T(8,128)(2,1)S(1)}, u32[]{:S(2)}, u32[]{:S(2)}) collective-permute-start(bf16[8,320,128]{2,1,0:T(8,128)(2,1)S(1)} %swap_cores.1), channel_id=1, source_target_pairs={{0,1},{1,0},{2,3},{3,2},{4,5},{5,4},{6,7},{7,6},{8,9},{9,8},{10,11... | collective-permute-start | bytes 1966088 | tf_op jit(solution)/shard_map/swap_cores/ppermute | solution.py:430
  37.9 3.1 %own_keys.1 = (bf16[4,512,256]{2,1,0:T(8,128)(2,1)S(1)}, bf16[4,512,256]{2,1,0:T(8,128)(2,1)S(1)}, f32[2048,256]{1,0:T(8,128)S(1)}, f32[2048,128]{1,0:T(8,128)S(1)}, bf16[1024,128]{1,0:T(8,128)(2,1)S(1)}) custom-call(bf16[8,848,128]{2,1,0:T(8,128)(2,1)S(1)} %all_to_all.20.r_ref), custom_call_target="tpu_custom_call" | custom-call | flops 4294967296 | bytes 8388608 | tf_op jit(solution)/shard_map/own_keys/pallas_call | solution.py:313
  41.0 0.0 collective-permute-done.o_ref
  41.0 0.0 copy-start
  41.0 4.2 %other_keys.1 = f32[16,6,128]{2,1,0:T(8,128)S(1)} custom-call(bf16[8,848,128]{2,1,0:T(8,128)(2,1)S(1)} %all_to_all.20.r_ref, bf16[8,320,128]{2,1,0:T(8,128)(2,1)S(1)} %collective-permute-done.o_ref, bf16[64,512]{1,0:T(8,128)(2,1)S(1)} %get-tuple-element.14.proj_ref, bf16[4,512,256]{2,1,0:T(8,128)(2,1)S(1)} %get-tuple-element.15.qs, ...), custom_call_target="tpu_custom_call" | custom-call | tf_op jit(solution)/shard_map/other_keys/pallas_call | solution.py:336
  45.2 10.0 %all_to_all.21.parts_ref = f32[16,6,128]{2,1,0:T(8,128)S(1)} all-to-all(f32[16,6,128]{2,1,0:T(8,128)S(1)} %other_keys.1), channel_id=1, replica_groups=mesh['dp'=32,'ctx'=16] {'ctx'}, dimensions={0} | all-to-all | bytes 98304 | tf_op jit(solution)/shard_map/exchange_parts/all_to_all | solution.py:437
  55.3 28.0 %all_to_all.22.every_ref = bf16[32,2,384]{2,1,0:T(2,128)(2,1)S(1)} all-to-all(bf16[32,2,384]{2,1,0:T(2,128)(2,1)S(1)} %get-tuple-element.21), channel_id=1, replica_groups=mesh['dp'=32,'ctx'=16] {'dp'}, dimensions={0} | all-to-all | bytes 98304 | tf_op jit(solution)/shard_map/exchange_documents/all_to_all | solution.py:451
  83.2 0.4 dots.1
  83.6 12.1 %all_to_all.23.all_ref = f32[16,8,128]{2,1,0:T(8,128)S(1)} all-to-all(f32[16,8,128]{2,1,0:T(8,128)S(1)} %dots.1), channel_id=1, replica_groups=mesh['dp'=32,'ctx'=16] {'ctx'}, dimensions={0} | all-to-all | bytes 131072 | tf_op jit(solution)/shard_map/exchange_slices/all_to_all | solution.py:461
  95.7 0.0 copy-done
  95.7 1.0 unit.1
  (2 shorter events, 0.1 us)
Async XLA Ops:
  32.6 8.4 %collective-permute-start = (bf16[8,320,128]{2,1,0:T(8,128)(2,1)S(1)}, bf16[8,320,128]{2,1,0:T(8,128)(2,1)S(1)}, u32[]{:S(2)}, u32[]{:S(2)}) collective-permute-start(bf16[8,320,128]{2,1,0:T(8,128)(2,1)S(1)} %swap_cores.1), channel_id=1, source_target_pairs={{0,1},{1,0},{2,3},{3,2},{4,5},{5,4},{6,7},{7,6},{8,9},{9,8},{10,11... | collective-permute-start | bytes 1966088 | tf_op jit(solution)/shard_map/swap_cores/ppermute | solution.py:430
  41.0 54.7 %copy-start = (s32[8]{0:T(128)S(1)}, s32[8]{0:T(128)}, u32[]{:S(2)}) copy-start(s32[8]{0:T(128)} %param.21) | copy-start | bytes 100

commit v7 on v6

--- a/solution.py
+++ b/solution.py
@@ -67,7 +67,7 @@
 
 def message_kernel(
     h_hbm, q_hbm, kv_hbm, o_hbm, d_hbm, lse_hbm, pin_hbm, pq_hbm, pk_hbm, pv_hbm, msg_ref, proj_ref,
-    h_ref, kv_ref, o_ref, d_ref, lse_ref, pin_ref, sems,
+    h_ref, q_ref, kv_ref, o_ref, d_ref, lse_ref, pin_ref, sems,
 ):
     tok = kv_ref.shape[0]
     heads = lse_ref.shape[0]
@@ -85,9 +85,7 @@
     deltas = len(todo)
     todo += [(pin_hbm, pin_ref)] + row_parts(h_hbm, h_ref, parts) + row_parts(kv_hbm, kv_ref, parts)
     inputs = len(todo)
-    for h in range(heads):
-        cols = pl.ds(h * HEAD_DIM, HEAD_DIM)
-        todo += [(q_hbm.at[:, cols], msg_ref.at[h // 2, pl.ds(Q_AT + (h % 2) * tok, tok), :])]
+    todo += row_parts(q_hbm, q_ref, parts)
     copies = start_all(todo, sems)
     for copy in copies[:deltas]:
         copy.wait()
@@ -124,6 +122,9 @@
         msg_ref[p, X_AT:T_AT, :] = x
     for copy in copies[inputs:]:
         copy.wait()
+    for h in range(heads):
+        at = Q_AT + h % 2 * tok
+        msg_ref[h // 2, at : at + tok, :] = q_ref[:, h * HEAD_DIM : (h + 1) * HEAD_DIM]
 
 
 def message_call(hidden_in, queries, keys_values, attn_out, out_grad, log_norms, proj_in_t, *proj_t):
@@ -139,9 +140,9 @@
         out_specs=(VMEM, VMEM),
         scratch_shapes=[
             pltpu.VMEM(a.shape, a.dtype)
-            for a in (hidden_in, keys_values, attn_out, out_grad, log_norms, proj_in_t)
+            for a in (hidden_in, queries, keys_values, attn_out, out_grad, log_norms, proj_in_t)
         ]
-        + [pltpu.SemaphoreType.DMA((13 + 2 * chips,))],
+        + [pltpu.SemaphoreType.DMA((15,))],
         compiler_params=pltpu.CompilerParams(vmem_limit_bytes=16 * 2**20),
     )(
         *[
@@ -277,8 +278,12 @@
     flat[pl.ds(1, rows, stride=3), :] = jnp.where(low_lanes, even_v, odd)
     flat[pl.ds(2, rows, stride=3), :] = jnp.where(low_lanes, odd, pltpu.roll(odd_v, RANK, 1))
     depth = out_ref.shape[1]
+    blocks = out_ref.shape[2] // LANES
+    slices = 3 * RANK // 2 // (depth * blocks)
     for i in range(out_ref.shape[0]):
-        out_ref[i] = flat[i * depth : (i + 1) * depth]
+        for j in range(blocks):
+            start = (i % slices * blocks + j) * depth
+            out_ref[i, :, j * LANES : (j + 1) * LANES] = flat[start : start + depth]
 
 
 def keys_kernel(r_ref, out_ref):
@@ -335,7 +340,7 @@
     half = 2 * LANES
     return pl.pallas_call(
         other_kernel,
-        out_shape=jax.ShapeDtypeStruct((2 * chips, 3 * RANK // 2 // (2 * chips), LANES), F32),
+        out_shape=jax.ShapeDtypeStruct((2 * chips, 4, 3 * RANK // 2 // chips // 4 * LANES), F32),
         in_specs=[VMEM] * 8,
         out_specs=VMEM,
         scratch_shapes=attention_scratch(rows, half) + [pltpu.VMEM((2 * rows, 2 * LANES), BF16)] * 3
@@ -360,30 +365,28 @@
     for i in range(1, parts_ref.shape[0]):
         mine = mine + parts_ref[i]
     mine_ref[...] = mine
-    rows = send_ref.shape[1]
-    wide = [mine[r : r + rows] for r in range(0, mine.shape[0], rows)]
-    send = jnp.concatenate(wide, axis=1).astype(BF16)
+    send = mine.astype(BF16)
     for i in range(send_ref.shape[0]):
         send_ref[i] = send
 
 
 def dot_kernel(mine_ref, every_ref, out_ref):
-    docs, rows, _ = every_ref.shape
+    docs, rows, width = every_ref.shape
     mine = mine_ref[...]
-    wide = jnp.concatenate([mine[r : r + rows] for r in range(0, mine.shape[0], rows)], axis=1)
     terms, squares = [], []
     for e in range(docs):
         other = every_ref[e].astype(F32)
-        for to, product in ((terms, wide * other), (squares, other * other)):
+        for to, product in ((terms, mine * other), (squares, other * other)):
             to.append(jnp.sum(product, axis=0, keepdims=True))
     terms = jnp.concatenate(terms + squares, axis=0)
     terms = sum(terms[:, i : i + LANES] for i in range(0, terms.shape[1], LANES))
     terms = jnp.concatenate([terms, jnp.zeros((LANES - 2 * docs, LANES), F32)], axis=0)
     ones = jnp.ones((8, LANES), BF16)
     sums = sum(nt(ones, t) for t in split3(terms))
-    depth = mine.shape[0]
+    depth = rows * (width // LANES)
     for i in range(out_ref.shape[0]):
-        out_ref[i, :depth] = mine
+        for j in range(width // LANES):
+            out_ref[i, j * rows : (j + 1) * rows] = mine[:, j * LANES : (j + 1) * LANES]
         out_ref[i, depth:] = sums[: out_ref.shape[1] - depth]
 
 
@@ -417,6 +420,7 @@
     heads = log_norms.shape[1]
     chips = heads // 2
     docs = lax.axis_size("dp")
+    same_x = [[chips * x + i for i in range(chips)] for x in range(2)]
     same_core = [[2 * p + c for p in range(chips)] for c in range(2)]
 
     with jax.named_scope("message"):
@@ -436,12 +440,11 @@
     with jax.named_scope("exchange_parts"):
         parts = lax.all_to_all(partial, "ctx", 0, 0, tiled=True)
     with jax.named_scope("sum_parts"):
-        depth = partial.shape[1]
         mine, send = pl.pallas_call(
             slice_kernel,
             out_shape=(
-                jax.ShapeDtypeStruct((depth, LANES), F32),
-                jax.ShapeDtypeStruct((docs, 2, depth // 2 * LANES), BF16),
+                jax.ShapeDtypeStruct(partial.shape[1:], F32),
+                jax.ShapeDtypeStruct((docs, *partial.shape[1:]), BF16),
             ),
             in_specs=[VMEM],
             out_specs=(VMEM, VMEM),
@@ -452,13 +455,13 @@
     with jax.named_scope("dots"):
         terms = pl.pallas_call(
             dot_kernel,
-            out_shape=jax.ShapeDtypeStruct((2 * chips, 8, LANES), F32),
+            out_shape=jax.ShapeDtypeStruct((chips, 16, LANES), F32),
             in_specs=[VMEM] * 2,
             out_specs=VMEM,
             compiler_params=small,
         )(mine, every)
     with jax.named_scope("exchange_slices"):
-        terms = lax.all_to_all(terms, "ctx", 0, 0, tiled=True)
+        terms = lax.all_to_all(terms, "ctx", 0, 0, axis_index_groups=same_x, tiled=True)
     with jax.named_scope("unit"):
         unit, scores = pl.pallas_call(
             functools.partial(unit_kernel, docs),

time: 97 us -> 95.7 us (0.987)
  blocking collectives: 79.5 us -> 78.3 us
    all_to_all x1, blocking collectives: 12.1 us -> 9.81 us  [local(): lax.all_to_all(terms, 'ctx', 0, 0, axis_index_groups=same_x, tiled=True)]
    all_to_all x1, blocking collectives: 28 us -> 29.1 us  [local(): every = lax.all_to_all(send, 'dp', 0, 0, tiled=True)]
where the time goes in v7:
time: 95.7 us; the launch traced here: 95.4 us
  blocking collectives  78.3 us (82%)
  Pallas kernels  11.1 us (12%)
  starting transfers between devices  5.3 us (6%)
    all_to_all x1, blocking collectives, local(): lax.all_to_all(msg, 'ctx', 0, 0, axis_index_groups=same_core, tiled=True)  29.4 us
    all_to_all x1, blocking collectives, local(): every = lax.all_to_all(send, 'dp', 0, 0, tiled=True)  29.1 us
    all_to_all x1, blocking collectives, local(): parts = lax.all_to_all(partial, 'ctx', 0, 0, tiled=True)  10 us
    all_to_all x1, blocking collectives, local(): lax.all_to_all(terms, 'ctx', 0, 0, axis_index_groups=same_x, tiled=True)  9.81 us
    ppermute x1, starting transfers between devices, local(): lax.ppermute(keys_call(got), 'ctx', [(i, i ^ 1) for i in range(2 * chips)])  5.3 us
    pallas_call x1, Pallas kernels, other_call(): pl.pallas_call(other_kernel, out_shape=jax.ShapeDtypeStruct((2 * chips, 4...  4.18 us
    pallas_call x1, Pallas kernels, own_call(): pl.pallas_call(own_kernel, out_shape=(jax.ShapeDtypeStruct((groups, 2 * h...  3.11 us
    pallas_call x1, Pallas kernels, message_call(): pl.pallas_call(message_kernel, out_shape=(jax.ShapeDtypeStruct((chips, TA...  2.44 us
  transfers between devices with their start and end apart: 1, of which 0 were waited for; matrix products, arithmetic and copies ran while one was open for 0% of the time, Pallas kernels for 3%

profile of v7, /device:TPU:1, one launch (start us, length us, event | category | flops | bytes accessed | tf_op | source)
XLA Modules:
  0.0 95.4 jit_solution(7204486035788721857)
XLA Ops:
  0.6 2.4 %message.1 = (bf16[8,848,128]{2,1,0:T(8,128)(2,1)S(1)}, bf16[64,512]{1,0:T(8,128)(2,1)S(1)}) custom-call(bf16[128,2560]{1,0:T(8,128)(2,1)} %bitcast.13, bf16[128,2048]{1,0:T(8,128)(2,1)} %bitcast.14, bf16[128,1024]{1,0:T(8,128)(2,1)} %bitcast.18, bf16[128,2048]{1,0:T(8,128)(2,1)} %bitcast.15, bf16[128,2048]{1,0:T(8,128)(2,1)} %bitcast.16, ...), custom_call_target="tpu_custom_call" | custom-call | tf_op jit(solution)/shard_map/message/pallas_call | solution.py:133
  3.1 29.4 %all_to_all.20.r_ref = bf16[8,848,128]{2,1,0:T(8,128)(2,1)S(1)} all-to-all(bf16[8,848,128]{2,1,0:T(8,128)(2,1)S(1)} %get-tuple-element.13), channel_id=1, replica_groups={{0,2,4,6,8,10,12,14},{1,3,5,7,9,11,13,15},{16,18,20,22,24,26,28,30},{17..., dimensions={0} | all-to-all | bytes 3473408 | tf_op jit(solution)/shard_map/exchange_heads/all_to_all | solution.py:432
  32.6 5.3 %collective-permute-start = (bf16[8,320,128]{2,1,0:T(8,128)(2,1)S(1)}, bf16[8,320,128]{2,1,0:T(8,128)(2,1)S(1)}, u32[]{:S(2)}, u32[]{:S(2)}) collective-permute-start(bf16[8,320,128]{2,1,0:T(8,128)(2,1)S(1)} %swap_cores.1), channel_id=1, source_target_pairs={{0,1},{1,0},{2,3},{3,2},{4,5},{5,4},{6,7},{7,6},{8,9},{9,8},{10,11... | collective-permute-start | bytes 1966088 | tf_op jit(solution)/shard_map/swap_cores/ppermute | solution.py:434
  37.9 3.1 %own_keys.1 = (bf16[4,512,256]{2,1,0:T(8,128)(2,1)S(1)}, bf16[4,512,256]{2,1,0:T(8,128)(2,1)S(1)}, f32[2048,256]{1,0:T(8,128)S(1)}, f32[2048,128]{1,0:T(8,128)S(1)}, bf16[1024,128]{1,0:T(8,128)(2,1)S(1)}) custom-call(bf16[8,848,128]{2,1,0:T(8,128)(2,1)S(1)} %all_to_all.20.r_ref), custom_call_target="tpu_custom_call" | custom-call | flops 4294967296 | bytes 8388608 | tf_op jit(solution)/shard_map/own_keys/pallas_call | solution.py:318
  41.0 0.0 collective-permute-done.o_ref
  41.0 0.0 copy-start
  41.0 4.2 %other_keys.1 = f32[16,4,384]{2,1,0:T(4,128)S(1)} custom-call(bf16[8,848,128]{2,1,0:T(8,128)(2,1)S(1)} %all_to_all.20.r_ref, bf16[8,320,128]{2,1,0:T(8,128)(2,1)S(1)} %collective-permute-done.o_ref, bf16[64,512]{1,0:T(8,128)(2,1)S(1)} %get-tuple-element.14.proj_ref, bf16[4,512,256]{2,1,0:T(8,128)(2,1)S(1)} %get-tuple-element.15.qs, ...), custom_call_target="tpu_custom_call" | custom-call | tf_op jit(solution)/shard_map/other_keys/pallas_call | solution.py:341
  45.2 10.0 %all_to_all.21.parts_ref = f32[16,4,384]{2,1,0:T(4,128)S(1)} all-to-all(f32[16,4,384]{2,1,0:T(4,128)S(1)} %other_keys.1), channel_id=1, replica_groups=mesh['dp'=32,'ctx'=16] {'ctx'}, dimensions={0} | all-to-all | bytes 196608 | tf_op jit(solution)/shard_map/exchange_parts/all_to_all | solution.py:441
  55.2 29.1 %all_to_all.22.every_ref = bf16[32,4,384]{2,1,0:T(4,128)(2,1)S(1)} all-to-all(bf16[32,4,384]{2,1,0:T(4,128)(2,1)S(1)} %get-tuple-element.21), channel_id=1, replica_groups=mesh['dp'=32,'ctx'=16] {'dp'}, dimensions={0} | all-to-all | bytes 196608 | tf_op jit(solution)/shard_map/exchange_documents/all_to_all | solution.py:454
  84.3 0.4 dots.1
  84.7 9.8 %all_to_all.23.all_ref = f32[8,16,128]{2,1,0:T(8,128)S(1)} all-to-all(f32[8,16,128]{2,1,0:T(8,128)S(1)} %dots.1), channel_id=1, replica_groups={{0,1,2,3,4,5,6,7},{8,9,10,11,12,13,14,15},{16,17,18,19,20,21,22,23},{24..., dimensions={0} | all-to-all | bytes 131072 | tf_op jit(solution)/shard_map/exchange_slices/all_to_all | solution.py:464
  94.5 0.0 copy-done
  94.5 0.9 unit.1
  (2 shorter events, 0.1 us)
Async XLA Ops:
  32.6 8.4 %collective-permute-start = (bf16[8,320,128]{2,1,0:T(8,128)(2,1)S(1)}, bf16[8,320,128]{2,1,0:T(8,128)(2,1)S(1)}, u32[]{:S(2)}, u32[]{:S(2)}) collective-permute-start(bf16[8,320,128]{2,1,0:T(8,128)(2,1)S(1)} %swap_cores.1), channel_id=1, source_target_pairs={{0,1},{1,0},{2,3},{3,2},{4,5},{5,4},{6,7},{7,6},{8,9},{9,8},{10,11... | collective-permute-start | bytes 1966088 | tf_op jit(solution)/shard_map/swap_cores/ppermute | solution.py:434
  41.0 53.5 %copy-start = (s32[8]{0:T(128)S(1)}, s32[8]{0:T(128)}, u32[]{:S(2)}) copy-start(s32[8]{0:T(128)} %param.21) | copy-start | bytes 100

commit v8 on v7

--- a/solution.py
+++ b/solution.py
@@ -231,15 +231,11 @@
         for_v, for_qk = group_terms(g, tok, seen_of, qs, ds, kx, kt, vt, ps, dss)
         for_v, for_qk = for_v + acc_v[to], for_qk + acc[to]
         for ref, val in ((rv, for_v), (rk, for_qk[:, LANES:]), (rq, for_qk[:, :LANES])):
-            high, low = split2(val)
+            val = val.astype(BF16)
             for h in range(2):
                 mine = slice(h * half, (h + 1) * half)
                 at = slice(h * rows + g * half, h * rows + (g + 1) * half)
-                ref[at, :LANES] = high[mine]
-                ref[at, LANES:] = low[mine]
-
-    def halves(a):
-        return a[:, :LANES] + a[:, LANES:]
+                ref[at, :] = val[mine]
 
     def exact(a, b, product):
         high, low = split2(a)
@@ -252,11 +248,11 @@
     mv = jnp.zeros((LANES, LANES), F32)
     for h in range(2):
         at = slice(h * rows, (h + 1) * rows)
-        mq = halves(tn(xl, rq[at])[:RANK])
+        mq = tn(xl, rq[at])[:RANK]
         pq = jnp.concatenate([proj_ref[:, h * HEAD_DIM : (h + 1) * HEAD_DIM], zero.astype(BF16)], axis=0)
         out_q = out_q + exact(mq, pq, nt)
-        mk = mk + halves(tn(part(r_ref, Q_AT + h * LANES), rk[at]))
-        mv = mv + halves(tn(part(r_ref, D_AT + h * LANES), rv[at]))
+        mk = mk + tn(part(r_ref, Q_AT + h * LANES), rk[at])
+        mv = mv + tn(part(r_ref, D_AT + h * LANES), rv[at])
     mk_high, mk_low = split2(mk)
     mv_high, mv_low = split2(mv)
     pk = proj_ref[:, 2 * HEAD_DIM : 3 * HEAD_DIM]
@@ -283,7 +279,7 @@
     for i in range(out_ref.shape[0]):
         for j in range(blocks):
             start = (i % slices * blocks + j) * depth
-            out_ref[i, :, j * LANES : (j + 1) * LANES] = flat[start : start + depth]
+            out_ref[i, :, j * LANES : (j + 1) * LANES] = flat[start : start + depth].astype(BF16)
 
 
 def keys_kernel(r_ref, out_ref):
@@ -340,10 +336,10 @@
     half = 2 * LANES
     return pl.pallas_call(
         other_kernel,
-        out_shape=jax.ShapeDtypeStruct((2 * chips, 4, 3 * RANK // 2 // chips // 4 * LANES), F32),
+        out_shape=jax.ShapeDtypeStruct((2 * chips, 4, 3 * RANK // 2 // chips // 4 * LANES), BF16),
         in_specs=[VMEM] * 8,
         out_specs=VMEM,
-        scratch_shapes=attention_scratch(rows, half) + [pltpu.VMEM((2 * rows, 2 * LANES), BF16)] * 3
+        scratch_shapes=attention_scratch(rows, half) + [pltpu.VMEM((2 * rows, LANES), BF16)] * 3
         + [pltpu.VMEM((2 * RANK, LANES), F32)],
         compiler_params=pltpu.CompilerParams(vmem_limit_bytes=24 * 2**20),
     )(got, other, proj, *saved)
@@ -361,9 +357,9 @@
 
 
 def slice_kernel(parts_ref, mine_ref, send_ref):
-    mine = parts_ref[0]
+    mine = parts_ref[0].astype(F32)
     for i in range(1, parts_ref.shape[0]):
-        mine = mine + parts_ref[i]
+        mine = mine + parts_ref[i].astype(F32)
     mine_ref[...] = mine
     send = mine.astype(BF16)
     for i in range(send_ref.shape[0]):

time: 95.7 us -> 95.4 us (level)
  no operation moved by 1% of the time
where the time goes in v8:
time: 95.4 us; the launch traced here: 95.1 us
  blocking collectives  78.2 us (82%)
  Pallas kernels  10.9 us (11%)
  starting transfers between devices  5.3 us (6%)
    all_to_all x1, blocking collectives, local(): lax.all_to_all(msg, 'ctx', 0, 0, axis_index_groups=same_core, tiled=True)  29.4 us
    all_to_all x1, blocking collectives, local(): every = lax.all_to_all(send, 'dp', 0, 0, tiled=True)  29 us
    all_to_all x1, blocking collectives, local(): parts = lax.all_to_all(partial, 'ctx', 0, 0, tiled=True)  9.97 us
    all_to_all x1, blocking collectives, local(): lax.all_to_all(terms, 'ctx', 0, 0, axis_index_groups=same_x, tiled=True)  9.83 us
    ppermute x1, starting transfers between devices, local(): lax.ppermute(keys_call(got), 'ctx', [(i, i ^ 1) for i in range(2 * chips)])  5.3 us
    pallas_call x1, Pallas kernels, other_call(): pl.pallas_call(other_kernel, out_shape=jax.ShapeDtypeStruct((2 * chips, 4...  3.96 us
    pallas_call x1, Pallas kernels, own_call(): pl.pallas_call(own_kernel, out_shape=(jax.ShapeDtypeStruct((groups, 2 * h...  3.11 us
    pallas_call x1, Pallas kernels, message_call(): pl.pallas_call(message_kernel, out_shape=(jax.ShapeDtypeStruct((chips, TA...  2.44 us
  transfers between devices with their start and end apart: 1, of which 0 were waited for; matrix products, arithmetic and copies ran while one was open for 0% of the time, Pallas kernels for 3%

profile of v8, /device:TPU:1, one launch (start us, length us, event | category | flops | bytes accessed | tf_op | source)
XLA Modules:
  0.0 95.1 jit_solution(10047922270194824103)
XLA Ops:
  0.6 2.4 %message.1 = (bf16[8,848,128]{2,1,0:T(8,128)(2,1)S(1)}, bf16[64,512]{1,0:T(8,128)(2,1)S(1)}) custom-call(bf16[128,2560]{1,0:T(8,128)(2,1)} %bitcast.13, bf16[128,2048]{1,0:T(8,128)(2,1)} %bitcast.14, bf16[128,1024]{1,0:T(8,128)(2,1)} %bitcast.18, bf16[128,2048]{1,0:T(8,128)(2,1)} %bitcast.15, bf16[128,2048]{1,0:T(8,128)(2,1)} %bitcast.16, ...), custom_call_target="tpu_custom_call" | custom-call | tf_op jit(solution)/shard_map/message/pallas_call | solution.py:133
  3.1 29.4 %all_to_all.20.r_ref = bf16[8,848,128]{2,1,0:T(8,128)(2,1)S(1)} all-to-all(bf16[8,848,128]{2,1,0:T(8,128)(2,1)S(1)} %get-tuple-element.13), channel_id=1, replica_groups={{0,2,4,6,8,10,12,14},{1,3,5,7,9,11,13,15},{16,18,20,22,24,26,28,30},{17..., dimensions={0} | all-to-all | bytes 3473408 | tf_op jit(solution)/shard_map/exchange_heads/all_to_all | solution.py:428
  32.6 5.3 %collective-permute-start = (bf16[8,320,128]{2,1,0:T(8,128)(2,1)S(1)}, bf16[8,320,128]{2,1,0:T(8,128)(2,1)S(1)}, u32[]{:S(2)}, u32[]{:S(2)}) collective-permute-start(bf16[8,320,128]{2,1,0:T(8,128)(2,1)S(1)} %swap_cores.1), channel_id=1, source_target_pairs={{0,1},{1,0},{2,3},{3,2},{4,5},{5,4},{6,7},{7,6},{8,9},{9,8},{10,11... | collective-permute-start | bytes 1966088 | tf_op jit(solution)/shard_map/swap_cores/ppermute | solution.py:430
  37.9 3.1 %own_keys.1 = (bf16[4,512,256]{2,1,0:T(8,128)(2,1)S(1)}, bf16[4,512,256]{2,1,0:T(8,128)(2,1)S(1)}, f32[2048,256]{1,0:T(8,128)S(1)}, f32[2048,128]{1,0:T(8,128)S(1)}, bf16[1024,128]{1,0:T(8,128)(2,1)S(1)}) custom-call(bf16[8,848,128]{2,1,0:T(8,128)(2,1)S(1)} %all_to_all.20.r_ref), custom_call_target="tpu_custom_call" | custom-call | flops 4294967296 | bytes 8388608 | tf_op jit(solution)/shard_map/own_keys/pallas_call | solution.py:314
  41.0 0.0 collective-permute-done.o_ref
  41.0 0.0 copy-start
  41.0 4.0 %other_keys.1 = bf16[16,4,384]{2,1,0:T(4,128)(2,1)S(1)} custom-call(bf16[8,848,128]{2,1,0:T(8,128)(2,1)S(1)} %all_to_all.20.r_ref, bf16[8,320,128]{2,1,0:T(8,128)(2,1)S(1)} %collective-permute-done.o_ref, bf16[64,512]{1,0:T(8,128)(2,1)S(1)} %get-tuple-element.14.proj_ref, bf16[4,512,256]{2,1,0:T(8,128)(2,1)S(1)} %get-tuple-element.15.qs, ...), custom_call_target="tpu_custom_call" | custom-call | tf_op jit(solution)/shard_map/other_keys/pallas_call | solution.py:337
  45.0 10.0 %all_to_all.21.parts_ref = bf16[16,4,384]{2,1,0:T(4,128)(2,1)S(1)} all-to-all(bf16[16,4,384]{2,1,0:T(4,128)(2,1)S(1)} %other_keys.1), channel_id=1, replica_groups=mesh['dp'=32,'ctx'=16] {'ctx'}, dimensions={0} | all-to-all | bytes 98304 | tf_op jit(solution)/shard_map/exchange_parts/all_to_all | solution.py:437
  55.0 29.0 %all_to_all.22.every_ref = bf16[32,4,384]{2,1,0:T(4,128)(2,1)S(1)} all-to-all(bf16[32,4,384]{2,1,0:T(4,128)(2,1)S(1)} %get-tuple-element.21), channel_id=1, replica_groups=mesh['dp'=32,'ctx'=16] {'dp'}, dimensions={0} | all-to-all | bytes 196608 | tf_op jit(solution)/shard_map/exchange_documents/all_to_all | solution.py:450
  84.0 0.4 dots.1
  84.3 9.8 %all_to_all.23.all_ref = f32[8,16,128]{2,1,0:T(8,128)S(1)} all-to-all(f32[8,16,128]{2,1,0:T(8,128)S(1)} %dots.1), channel_id=1, replica_groups={{0,1,2,3,4,5,6,7},{8,9,10,11,12,13,14,15},{16,17,18,19,20,21,22,23},{24..., dimensions={0} | all-to-all | bytes 131072 | tf_op jit(solution)/shard_map/exchange_slices/all_to_all | solution.py:460
  94.2 0.0 copy-done
  94.2 0.9 unit.1
  (2 shorter events, 0.1 us)
Async XLA Ops:
  32.6 8.4 %collective-permute-start = (bf16[8,320,128]{2,1,0:T(8,128)(2,1)S(1)}, bf16[8,320,128]{2,1,0:T(8,128)(2,1)S(1)}, u32[]{:S(2)}, u32[]{:S(2)}) collective-permute-start(bf16[8,320,128]{2,1,0:T(8,128)(2,1)S(1)} %swap_cores.1), channel_id=1, source_target_pairs={{0,1},{1,0},{2,3},{3,2},{4,5},{5,4},{6,7},{7,6},{8,9},{9,8},{10,11... | collective-permute-start | bytes 1966088 | tf_op jit(solution)/shard_map/swap_cores/ppermute | solution.py:430
  41.0 53.2 %copy-start = (s32[8]{0:T(128)S(1)}, s32[8]{0:T(128)}, u32[]{:S(2)}) copy-start(s32[8]{0:T(128)} %param.21) | copy-start | bytes 100
